TPU v7x, 32 devices: a whole 2x2x4 slice. The times are simulated.
32 devices in a mesh: group: 2 (over x), lat: 8 (over z, y), spec: 2 (over core).
Axes of the slice: x: 2, y: 2, z: 4, core: 2. Of those that a mesh axis runs over, the one named last changes fastest.
Arguments:
- field_grid: float32 [2, 32, 64, 3600], P(None, 'lat', ('group', 'spec')), parts along dimension 2, may hold values from -6 to 6
- quad_weight: float32 [32], P('lat'), may hold values from 0.5 to 2
- owner_waves: int32 [2, 8, 2], replicated, may hold values from 0 to 1800, as said below
- skip_blocks: int32 [8, 2, 8, 2], replicated, may hold values from 0 to 3
- legendre_table: bfloat16 [2, 8, 30, 32, 64], P('spec', None, None, 'lat'), may hold values from -24 to 24
- given_spectrum: bfloat16 [2, 8, 30, 2, 64, 64], P('spec', 'lat', None, None, 'group'), parts along dimension 4, may hold values from -6 to 6
Outputs:
- spectrum: float32 [2, 8, 30, 2, 64, 64], P('spec', 'lat', None, None, 'group'), parts along dimension 4
- back_grid: float32 [2, 32, 64, 3600], P(None, 'lat', ('group', 'spec')), parts along dimension 2
There are 2 independent parts, one for each index of `group`. A program takes and returns all parts, laid end to end along the dimension named above; an argument that names none is the same for every part. Nothing has to cross between parts.
Inputs may be any that keep to these rules, and one draw needn't show every extreme that they name: `owner_waves`: row (h, o) holds a wavenumber m below 900 and then its partner 1800 - m; all wavenumbers are distinct, and 0 and 1800 are among them.
All inputs are finite; a program needn't handle non-finite values.
Results may differ from a plain program's by a relative error of at most 0.0029.
Values may be sent and summed in bfloat16 or wider, within the bound.
A program may use at most 256 MiB of HBM per device.

v0:
```python
import math

import jax
import jax.numpy as jnp
from jax import lax
from jax.sharding import PartitionSpec as P

L = 1800
KB = 64


def fourier_table(owner_waves, length):
    wave_list = owner_waves.reshape(-1)
    grid_points = jnp.arange(length, dtype=jnp.int32)
    phase_index = grid_points[:, None] * wave_list[None, :] % length
    angles = phase_index.astype(jnp.float32) * (2.0 * math.pi / length)
    return jnp.concatenate([jnp.cos(angles), -jnp.sin(angles)], axis=1)


def legendre_mask(block_table, pair_waves, pair_skip):
    block_counts = (L + KB - pair_waves) // KB
    slot_index = jnp.arange(block_table.shape[1], dtype=jnp.int32)
    slot_start = jnp.stack([jnp.zeros_like(block_counts[:, 0]), block_counts[:, 0]], axis=1)
    block_index = slot_index[None, :, None] - slot_start[:, None, :]
    inside = (block_index >= 0) & (block_index < block_counts[:, None, :])
    degree = (
        pair_waves[:, None, :, None]
        + KB * block_index[:, :, :, None]
        + jnp.arange(KB, dtype=jnp.int32)
    )
    inside = inside[:, :, :, None] & (degree <= L)
    not_skipped = block_index[:, :, :, None] >= jnp.transpose(pair_skip, (1, 2, 0))[:, None, :, :]
    keep_mask = inside[:, :, :, None, :] & not_skipped[:, :, :, :, None]
    return jnp.where(keep_mask, block_table[:, :, None, :, :], jnp.zeros((), block_table.dtype))


def spread_parity(folded, degrees):
    parity = (jnp.arange(degrees, dtype=jnp.int32) % 2)[None, None, None, :, None, None]
    even_part = folded[:, :, :, 0][:, :, :, None]
    odd_part = folded[:, :, :, 1][:, :, :, None]
    return jnp.where(parity == 0, even_part, odd_part)


def forward_terms(masked, folded):
    degree_fold = spread_parity(folded, masked.shape[4])
    return jnp.einsum(
        "nksji,jnsirc->nkrci", masked, degree_fold, preferred_element_type=jnp.float32
    )


def adjoint_terms(masked, coeffs):
    per_degree = jnp.einsum(
        "nksji,nkrci->jnsirc", masked, coeffs, preferred_element_type=jnp.float32
    )
    shape_now = per_degree.shape
    split_degree = per_degree.reshape(shape_now[:3] + (shape_now[3] // 2, 2) + shape_now[4:])
    return jnp.sum(split_degree, axis=3)


def fold_forward(fourier, quad_weight):
    symmetric = fourier[0] + fourier[1]
    antisymmetric = fourier[0] - fourier[1]
    stacked = (
        jnp.stack([symmetric, antisymmetric], axis=-1) * quad_weight[:, None, None, None, None]
    )
    stacked = stacked.astype(jnp.bfloat16)
    pair_count, channels, part_count, wave_count, parity = stacked.shape
    shaped = stacked.reshape(pair_count, channels, part_count, wave_count // 2, 2, parity)
    return jnp.transpose(shaped, (0, 3, 4, 5, 2, 1))


def fold_adjoint(synthesis, quad_weight):
    north_part = synthesis[:, :, :, 0] + synthesis[:, :, :, 1]
    south_part = synthesis[:, :, :, 0] - synthesis[:, :, :, 1]
    stacked = (
        jnp.stack([north_part, south_part], axis=0) * quad_weight[None, :, None, None, None, None]
    )
    hemispheres, pair_count, owner_count, slots_two, part_count, channels = stacked.shape
    moved = jnp.transpose(stacked, (0, 1, 5, 4, 2, 3))
    return moved.reshape(hemispheres, pair_count, channels, part_count, owner_count * slots_two)


def on_device(field_grid, quad_weight, owner_waves, skip_blocks, legendre_table, given_spectrum):
    length = field_grid.shape[3]
    wave_table = fourier_table(owner_waves, length)
    wave_count = wave_table.shape[1] // 2
    flat_rows = field_grid.reshape(-1, length)
    fourier = jnp.dot(
        flat_rows, wave_table, precision=lax.Precision.HIGHEST, preferred_element_type=jnp.float32
    ) * (1.0 / length)
    fourier = fourier.reshape(field_grid.shape[:3] + (2, wave_count))
    fourier = lax.all_to_all(fourier, "spec", split_axis=4, concat_axis=2, tiled=True)
    folded = fold_forward(fourier, quad_weight)
    spec_index = lax.axis_index("spec")
    band_index = lax.axis_index("lat")
    my_waves = lax.dynamic_index_in_dim(owner_waves, spec_index, 0, keepdims=False)
    pair_count = field_grid.shape[1]
    owner_count = my_waves.shape[0]
    band_skips = lax.dynamic_index_in_dim(skip_blocks, band_index, 0, keepdims=False)
    my_skips = lax.dynamic_index_in_dim(band_skips, spec_index, 0, keepdims=False)
    pair_skip = jnp.broadcast_to(my_skips[None], (pair_count, owner_count, 2))
    masked = legendre_mask(legendre_table[0], my_waves, pair_skip)
    part_mask = masked
    spectrum = lax.psum_scatter(
        forward_terms(part_mask, folded), "lat", scatter_dimension=0, tiled=True
    )
    part_mask = masked
    values = adjoint_terms(part_mask, lax.all_gather(given_spectrum, "lat", axis=1, tiled=True)[0])
    spectrum = spectrum.reshape(given_spectrum.shape)
    back_fourier = fold_adjoint(values, quad_weight)
    back_fourier = lax.all_to_all(back_fourier, "spec", split_axis=2, concat_axis=4, tiled=True)
    back_rows = back_fourier.reshape(-1, 2 * wave_count)
    back_grid = jnp.dot(
        back_rows, wave_table.T, precision=lax.Precision.HIGHEST, preferred_element_type=jnp.float32
    ) * (1.0 / length)
    return (spectrum, back_grid.reshape(field_grid.shape))


def solution(mesh):
    return jax.shard_map(
        on_device,
        mesh=mesh,
        in_specs=(
            P(None, "lat", ("group", "spec"), None),
            P("lat"),
            P(),
            P(),
            P("spec", None, None, "lat", None),
            P("spec", "lat", None, None, "group", None),
        ),
        out_specs=(
            P("spec", "lat", None, None, "group", None),
            P(None, "lat", ("group", "spec"), None),
        ),
        check_vma=False,
    )
```

profile of v0, /device:TPU:0, one launch (start us, length us, event | category | flops | bytes accessed | tf_op | source)
XLA Modules:
  0.0 378.7 jit_solution(6509203041263984998)
XLA Ops:
  7.2 0.7 all-gather.2.cloned.1.call-update
  7.9 0.8 copy.92
  8.8 2.0 fusion.23
  10.8 2.0 fusion.4
  13.3 0.8 reshape.179
  14.1 3.3 all-to-all-start
  17.7 1.0 all-to-all-done
  18.7 0.5 broadcast.141
  19.2 0.7 reduce
  21.1 0.7 dynamic-slice_bitcast_fusion
  22.1 1.3 copy.102
  23.7 0.4 compare_and_fusion
  24.1 0.7 copy-done.1
  24.8 7.6 %convolution_bitcast_fusion = f32[8,30,2,32,64]{1,3,2,4,0:T(8,128)} fusion(pred[64]{0:T(512)(128)(4,1)S(1)} %fusion.28, bf16[4,8,2,2,32]{4,0,2,3,1:T(4,128)(2,1)S(1)} %copy.97, bf16[4,8,2,2,32]{4,0,2,3,1:T(4,128)(2,1)S(1)} %copy.96, pred[8,30,2,4]{1,3,2,0:T(4,128)(4,1)S(1)} %broadcast_compare_fusion, pred[8,30,2,64]{1,2,3,0:T(4,128)(4,1)S(1)} %compare_and_fusion, ...), kind=kOutput, calls=%fused_computation | convolution fusion | flops 16236544 | bytes 4104128 | tf_op jit(solution)/shard_map/nksji,jnsirc->nkrci/dot_general | solution.py:46
  32.5 50.6 %all-gather.2.cloned.1.call-done = bf16[1,8,30,2,32,64]{5,4,3,2,0,1:T(8,128)(2,1)} async-done(((bf16[1,1,30,2,32,64]{5,4,3,2,0,1:T(8,128)(2,1)}), bf16[1,8,30,2,32,64]{5,4,3,2,0,1:T(8,128)(2,1)}) %all-gather.2.cloned.1.call-update) | async-done | bytes 1966096 | tf_op jit(solution)/shard_map/all_gather | solution.py:108
  83.0 13.4 %copy.104 = bf16[1,8,30,2,32,64]{4,2,3,5,1,0:T(8,128)(2,1)} copy(bf16[1,8,30,2,32,64]{5,4,3,2,0,1:T(8,128)(2,1)} %all-gather.2.cloned.1.call-done) | data formatting | bytes 3932160 | tf_op jit(solution)/shard_map/all_gather | solution.py:108
  96.4 7.4 %fusion = f32[8,64,2,4,2,32]{5,3,4,2,1,0:T(4,128)} fusion(bf16[1,8,30,2,32,64]{4,2,3,5,1,0:T(8,128)(2,1)} %copy.104, pred[8,30,2,4]{1,3,2,0:T(4,128)(4,1)S(1)} %broadcast_compare_fusion, pred[8,30,2,64]{1,2,3,0:T(4,128)(4,1)} %copy-done.1, bf16[8,30,4,64]{1,2,3,0:T(4,128)(2,1)S(1)} %copy.102), kind=kOutput, calls=%fused_computation.1 | convolution fusion | flops 15974400 | bytes 3170176 | tf_op jit(solution)/shard_map/nksji,nkrci->jnsirc/dot_general | solution.py:52
  103.8 3.3 reduce_sum.9
  107.9 3.7 all_to_all.30
  111.6 0.7 reduce.1
  113.2 4.3 %convolution_multiply_fusion = f32[128,3600]{0,1:T(8,128)} fusion(f32[128,64]{0,1:T(8,128)S(1)} %reshape.174, f32[3600,32]{0,1:T(8,128)S(1)} %get-tuple-element.23, f32[3600,32]{0,1:T(8,128)S(1)} %get-tuple-element.22), kind=kOutput, calls=%fused_computation.3 | convolution fusion | flops 354585600 | bytes 2797568 | tf_op jit(solution)/shard_map/dot_general | solution.py:113
  117.5 2.8 copy.111
  120.3 247.7 %reduce-scatter.2.cloned.1.call-done = f32[1,30,2,32,64]{1,3,2,4,0:T(8,128)} async-done(((f32[8,30,2,32,64]{1,3,2,4,0:T(8,128)}), f32[1,30,2,32,64]{1,3,2,4,0:T(8,128)}) %reduce-scatter.2.cloned.1.call-update) | async-done | bytes 491536 | tf_op jit(solution)/shard_map/reduce_scatter | solution.py:104
  368.0 3.9 %copy.112 = f32[1,1,30,2,32,64]{5,4,3,2,1,0:T(8,128)} copy(f32[1,1,30,2,32,64]{2,4,3,5,1,0:T(8,128)} %bitcast.78) | data formatting | bytes 983040
  (42 shorter events, 4.0 us)
Async XLA Ops:
  7.2 3.6 copy-start
  7.2 75.9 %all-gather.2.cloned.1.call-start = ((), (), s32[]{:S(2)}) async-start(), calls=%async_computation.4 | async-start | bytes 4423680 | tf_op jit(solution)/shard_map/all_gather | solution.py:108
  10.8 6.8 %copy-start.2 = (s32[2,8,2]{1,2,0:T(2,128)S(1)}, s32[2,8,2]{1,2,0:T(2,128)}, u32[]{:S(2)}) copy-start(s32[2,8,2]{1,2,0:T(2,128)} %param.8) | copy-start | bytes 388
  12.8 8.0 %copy-start.3 = (f32[4]{0:T(128)S(1)}, f32[4]{0:T(128)}, u32[]{:S(2)}) copy-start(f32[4]{0:T(128)} %param.7) | copy-start | bytes 52
  14.1 4.6 %all-to-all-start = ((f32[2,1,4096]{2,1,0:T(1,128)}), f32[2,1,4096]{2,1,0:T(1,128)S(1)}, u32[]{:S(2)}, u32[]{:S(2)}) async-start(f32[2,1,4096]{2,1,0:T(1,128)} %reshape.179), calls=%async_computation | async-start | bytes 65536 | tf_op jit(solution)/shard_map/all_to_all | solution.py:92
  17.4 350.7 %reduce-scatter.2.cloned.1.call-start = ((), (), s32[]{:S(2)}) async-start(), calls=%async_computation.3 | async-start | bytes 18874368 | tf_op jit(solution)/shard_map/reduce_scatter | solution.py:104
  24.1 0.7 copy-start.1
Sparse Core Ops, SparseCore 0:
  10.2 72.7 all-gather.1
  86.8 281.1 reduce-scatter.1
where the time goes:
time: 379 us
  waiting for transfers between devices  300 us (79%)
  local copies, waits for them, and re-layouts  28 us (7%)
  matrix products  21.4 us (6%)
  between operations  14.3 us (4%)
  other arithmetic  7.79 us (2%)
    reduce_scatter x1, waiting for transfers between devices, on_device(): lax.psum_scatter(forward_terms(part_mask, folded), 'lat', scatter_dimensi...  248 us
    all_gather x1, waiting for transfers between devices, on_device(): lax.all_gather(given_spectrum, 'lat', axis=1, tiled=True)[0]  50.6 us
    all_gather x1, local copies, waits for them, and re-layouts, on_device(): lax.all_gather(given_spectrum, 'lat', axis=1, tiled=True)[0]  13.4 us
    dot_general x1, matrix products, forward_terms(): jnp.einsum('nksji,jnsirc->nkrci', masked, degree_fold, preferred_element_...  7.63 us
  transfers between devices with their start and end apart: 3, of which 3 were waited for; matrix products, arithmetic and copies ran while one was open for 14% of the time, Pallas kernels for 0%

commit v1 on v0

v1 whole, which is shorter than its diff:
```python
import math

import jax
import jax.numpy as jnp
from jax import lax
from jax.sharding import PartitionSpec as P

L = 1800
KB = 64


def fourier_table(owner_waves, length):
    wave_list = owner_waves.reshape(-1)
    grid_points = jnp.arange(length, dtype=jnp.int32)
    phase_index = grid_points[:, None] * wave_list[None, :] % length
    angles = phase_index.astype(jnp.float32) * (2.0 * math.pi / length)
    return jnp.concatenate([jnp.cos(angles), -jnp.sin(angles)], axis=1)


def owner_table(blocks, waves, skips, pair_dev):
    slots, pairs, degrees = blocks.shape
    counts = (L + KB - waves) // KB
    starts = jnp.stack([jnp.zeros_like(counts[0]), counts[0]])
    block = jnp.arange(slots, dtype=jnp.int32)[None, :] - starts[:, None]
    inside = (block >= 0) & (block < counts[:, None])
    ramp = jnp.arange(degrees, dtype=jnp.int32)
    inside = inside[:, :, None] & (waves[:, None, None] + KB * block[:, :, None] + ramp <= L)
    skip_rows = jnp.repeat(skips.T, pair_dev, axis=1)
    stored = block[:, None, :] >= skip_rows[:, :, None]
    keep = inside[:, None, None] & stored[:, :, None, :, None]
    keep = keep & (ramp % 2 == jnp.arange(2)[:, None])[None, None, :, None, :]
    moved = jnp.transpose(blocks, (1, 0, 2))[None, :, None]
    return jnp.where(keep, moved, jnp.zeros((), blocks.dtype))


def on_device(
    lat_count, spec_count, field_grid, quad_weight, owner_waves, skip_blocks, legendre_table, given_spectrum
):
    hemispheres, pair_dev, channels, length = field_grid.shape
    table_blocks = lax.all_to_all(legendre_table[0], "lat", split_axis=0, concat_axis=2, tiled=True)[0]
    wave_table = fourier_table(owner_waves, length)
    wave_count = wave_table.shape[1] // 2
    fourier = jnp.dot(
        field_grid.reshape(-1, length),
        wave_table,
        precision=lax.Precision.HIGHEST,
        preferred_element_type=jnp.float32,
    ) * (1.0 / length)
    fourier = fourier.reshape(hemispheres, pair_dev, channels, 2, wave_count)
    weight = quad_weight[:, None, None, None]
    folded = jnp.stack(
        [(fourier[0] + fourier[1]) * weight, (fourier[0] - fourier[1]) * weight], axis=1
    ).astype(jnp.bfloat16)
    folded = folded.reshape(pair_dev, 2, channels, 2, wave_count // 2, 2)
    folded = jnp.transpose(folded, (4, 0, 5, 1, 3, 2))
    folded = lax.all_to_all(folded, ("spec", "lat"), split_axis=0, concat_axis=0, tiled=True)
    folded = folded.reshape(spec_count, lat_count, pair_dev, 2, 2, 2, channels)
    folded = jnp.transpose(folded, (3, 1, 2, 4, 5, 0, 6))
    rows = 2 * lat_count * pair_dev * 2
    columns = 2 * spec_count * channels
    folded = folded.reshape(rows, columns)

    spec_index = lax.axis_index("spec")
    lat_index = lax.axis_index("lat")
    waves = owner_waves[spec_index, lat_index]
    skips = skip_blocks[:, spec_index, lat_index]
    masked = owner_table(table_blocks, waves, skips, pair_dev)
    masked = masked.reshape((rows,) + masked.shape[3:])
    coeffs = given_spectrum[0, 0].reshape(given_spectrum.shape[2], columns, KB)
    synthesis = jnp.einsum("qki,kxi->qx", masked, coeffs, preferred_element_type=jnp.float32)
    spectrum = jnp.einsum("qki,qx->kxi", masked, folded, preferred_element_type=jnp.float32)

    synthesis = synthesis.reshape(2, lat_count, pair_dev, 2, 2, spec_count, channels)
    synthesis = jnp.transpose(synthesis, (5, 1, 2, 0, 3, 4, 6)).reshape(
        spec_count * lat_count, pair_dev, 2, 2, 2, channels
    )
    synthesis = lax.all_to_all(synthesis, ("spec", "lat"), split_axis=0, concat_axis=0, tiled=True)
    back = jnp.stack(
        [synthesis[:, :, :, 0] + synthesis[:, :, :, 1], synthesis[:, :, :, 0] - synthesis[:, :, :, 1]]
    ) * quad_weight[None, None, :, None, None, None]
    back = jnp.transpose(back, (0, 2, 5, 4, 1, 3)).reshape(-1, 2 * wave_count)
    back_grid = jnp.dot(
        back, wave_table.T, precision=lax.Precision.HIGHEST, preferred_element_type=jnp.float32
    ) * (1.0 / length)
    return (spectrum.reshape(given_spectrum.shape), back_grid.reshape(field_grid.shape))


def solution(mesh):
    lat_count, spec_count = mesh.shape["lat"], mesh.shape["spec"]

    def body(*args):
        return on_device(lat_count, spec_count, *args)

    return jax.shard_map(
        body,
        mesh=mesh,
        in_specs=(
            P(None, "lat", ("group", "spec"), None),
            P("lat"),
            P(),
            P(),
            P("spec", None, None, "lat", None),
            P("spec", "lat", None, None, "group", None),
        ),
        out_specs=(
            P("spec", "lat", None, None, "group", None),
            P(None, "lat", ("group", "spec"), None),
        ),
        check_vma=False,
    )
```

time: 379 us -> 60.9 us (0.16)
  waiting for transfers between devices: 300 us -> 14.7 us
  local copies, waits for them, and re-layouts: 28 us -> 13 us
  between operations: 14.3 us -> 0.98 us
  matrix products: 21.4 us -> 9.59 us
  starting transfers between devices: 3.52 us -> 15 us
    reduce_scatter x1 -> x0, waiting for transfers between devices: 248 us -> none  [on_device(): lax.psum_scatter(forward_terms(part_mask, folded), 'lat', scatter_dimensi...]
    all_gather x1 -> x0, waiting for transfers between devices: 50.6 us -> none  [on_device(): lax.all_gather(given_spectrum, 'lat', axis=1, tiled=True)[0]]
    all_to_all x1 -> x3, waiting for transfers between devices: 1.01 us -> 14.7 us  [the longest x1 6.36 us: on_device(): lax.all_to_all(legendre_table[0], 'lat', split_axis=0, concat_axis=2, til...]
    all_gather x1 -> x0, local copies, waits for them, and re-layouts: 13.4 us -> none  [on_device(): lax.all_gather(given_spectrum, 'lat', axis=1, tiled=True)[0]]
    all_to_all x1 -> x3, starting transfers between devices: 3.26 us -> 15 us  [the longest x1 7.39 us: on_device(): lax.all_to_all(folded, ('spec', 'lat'), split_axis=0, concat_axis=0, tile...]
    dot_general x4, matrix products: 21.4 us -> 9.59 us  [the longest x1 4.35 us: on_device(): jnp.dot(back, wave_table.T, precision=lax.Precision.HIGHEST, preferred_el...]
  transfers between devices with their start and end apart: 3 -> 3, of which waited for: 3 -> 3; matrix products, arithmetic and copies ran while one was open for 14% -> 9% of each run, Pallas kernels for 0% -> 0%
where the time goes in v1:
time: 60.9 us; the launch traced here: 60.4 us
  starting transfers between devices  15 us (25%)
  waiting for transfers between devices  14.7 us (24%)
  local copies, waits for them, and re-layouts  13 us (21%)
  matrix products  9.59 us (16%)
  other arithmetic  7.02 us (12%)
  between operations  0.98 us (2%)
    all_to_all x1, starting transfers between devices, on_device(): lax.all_to_all(folded, ('spec', 'lat'), split_axis=0, concat_axis=0, tile...  7.39 us
    all_to_all x1, waiting for transfers between devices, on_device(): lax.all_to_all(legendre_table[0], 'lat', split_axis=0, concat_axis=2, til...  6.36 us
    unnamed x20, local copies, waits for them, and re-layouts  5.7 us
    all_to_all x1, waiting for transfers between devices, on_device(): lax.all_to_all(folded, ('spec', 'lat'), split_axis=0, concat_axis=0, tile...  4.55 us
    dot_general x1, matrix products, on_device(): jnp.dot(back, wave_table.T, precision=lax.Precision.HIGHEST, preferred_el...  4.35 us
    all_to_all x1, starting transfers between devices, on_device(): lax.all_to_all(legendre_table[0], 'lat', split_axis=0, concat_axis=2, til...  4 us
    all_to_all x1, waiting for transfers between devices, on_device(): lax.all_to_all(synthesis, ('spec', 'lat'), split_axis=0, concat_axis=0, t...  3.83 us
    all_to_all x1, starting transfers between devices, on_device(): lax.all_to_all(synthesis, ('spec', 'lat'), split_axis=0, concat_axis=0, t...  3.66 us
  transfers between devices with their start and end apart: 3, of which 3 were waited for; matrix products, arithmetic and copies ran while one was open for 9% of the time, Pallas kernels for 0%

profile of v1, /device:TPU:0, one launch (start us, length us, event | category | flops | bytes accessed | tf_op | source)
XLA Modules:
  0.0 60.4 jit_solution(17578944766678486321)
XLA Ops:
  0.6 0.9 %copy.103 = s32[2,8,2]{2,1,0:T(8,128)S(1)} copy(s32[2,8,2]{1,2,0:T(2,128)} %param.8) | data formatting | bytes 256 | tf_op args[2]
  1.6 2.0 %fusion.8 = (f32[3600,32]{0,1:T(8,128)S(1)}, f32[3600,32]{0,1:T(8,128)S(1)}) fusion(s32[32]{0:T(128)S(1)} %mul.86), kind=kLoop, calls=%fused_computation.18 | loop fusion | flops 1152000 | bytes 921728 | tf_op jit(solution)/shard_map/cos | solution.py:17
  3.7 2.0 %fusion.1 = f32[128,64]{0,1:T(8,128)S(1)} fusion(f32[128,3600]{1,0:T(8,128)S(1)} %bitcast.80, f32[3600,32]{0,1:T(8,128)S(1)} %get-tuple-element.9, f32[3600,32]{0,1:T(8,128)S(1)} %get-tuple-element.8), kind=kOutput, calls=%fused_computation.6 | convolution fusion | flops 354132992 | bytes 2797568 | tf_op jit(solution)/shard_map/dot_general | solution.py:43
  6.7 0.8 %reshape.318 = bf16[16,2,256]{2,1,0:T(2,128)(2,1)} reshape(bf16[16,4,2,2,2,16]{5,4,3,2,1,0:T(2,128)(2,1)S(1)} %copy.106) | data formatting | bytes 32768
  7.4 7.4 %all-to-all-start = ((bf16[16,2,256]{2,1,0:T(2,128)(2,1)}), bf16[16,2,256]{2,1,0:T(2,128)(2,1)S(1)}, u32[]{:S(2)}, u32[]{:S(2)}) async-start(bf16[16,2,256]{2,1,0:T(2,128)(2,1)} %reshape.318), calls=%async_computation | async-start | bytes 32768 | tf_op jit(solution)/shard_map/all_to_all | solution.py:56
  15.9 0.8 %reshape.316 = bf16[8,2,3840]{2,1,0:T(2,128)(2,1)} reshape(bf16[8,30,4,64]{3,2,1,0:T(4,128)(2,1)S(1)} %bitcast.93) | data formatting | bytes 245760
  16.7 4.6 %all-to-all-done = bf16[16,2,256]{2,1,0:T(2,128)(2,1)S(1)} async-done(((bf16[16,2,256]{2,1,0:T(2,128)(2,1)}), bf16[16,2,256]{2,1,0:T(2,128)(2,1)S(1)}, u32[]{:S(2)}, u32[]{:S(2)}) %all-to-all-start) | async-done | bytes 16416 | tf_op jit(solution)/shard_map/all_to_all | solution.py:56
  21.3 4.0 %all-to-all-start.1 = ((bf16[8,2,3840]{2,1,0:T(2,128)(2,1)}), bf16[8,2,3840]{2,1,0:T(2,128)(2,1)}, u32[]{:S(2)}, u32[]{:S(2)}) async-start(bf16[8,2,3840]{2,1,0:T(2,128)(2,1)} %reshape.316), calls=%async_computation.1 | async-start | bytes 245760 | tf_op jit(solution)/shard_map/all_to_all | solution.py:40
  25.3 0.3 broadcast_and_fusion
  26.2 6.4 %all-to-all-done.1 = bf16[8,2,3840]{2,1,0:T(2,128)(2,1)} async-done(((bf16[8,2,3840]{2,1,0:T(2,128)(2,1)}), bf16[8,2,3840]{2,1,0:T(2,128)(2,1)}, u32[]{:S(2)}, u32[]{:S(2)}) %all-to-all-start.1) | async-done | bytes 122912 | tf_op jit(solution)/shard_map/all_to_all | solution.py:40
  32.6 1.8 %reshape.317 = bf16[8,30,4,64]{3,2,1,0:T(4,128)(2,1)} reshape(bf16[8,2,3840]{2,1,0:T(2,128)(2,1)} %all-to-all-done.1) | data formatting | bytes 245760
  34.4 1.0 %copy.110 = bf16[1,30,8,4,64]{4,3,2,1,0:T(4,128)(2,1)S(1)} copy(bf16[1,30,8,4,64]{4,3,1,2,0:T(4,128)(2,1)} %bitcast.91) | data formatting | bytes 245760 | tf_op jit(solution)/shard_map/all_to_all | solution.py:40
  35.4 2.4 %and_select_fusion = bf16[2,32,2,30,64]{4,2,1,0,3:T(2,128)(2,1)} fusion(pred[2,64]{1,0:T(4,128)(4,1)S(1)} %iota_compare_fusion, pred[2,32,30,64]{3,1,0,2:T(8,128)(4,1)S(1)} %broadcast_and_fusion, bf16[32,30,64]{2,0,1:T(8,128)(2,1)S(1)} %bitcast.85), kind=kLoop, calls=%fused_computation.1 | loop fusion | flops 491520 | bytes 737408 | tf_op jit(solution)/shard_map/jit(_where)/select_n | solution.py:33
  37.8 0.9 %broadcast_in_dim.15 = bf16[2,32,2,30,64]{4,2,1,0,3:T(2,128)(2,1)S(1)} broadcast(bf16[32,30,64]{2,0,1:T(8,128)(2,1)S(1)} %bitcast.86), dimensions={1,3,4} | broadcast | bytes 614400 | tf_op jit(solution)/shard_map/jit(_where)/broadcast_in_dim | solution.py:33
  38.7 0.9 %fusion = bf16[128,30,64]{2,1,0:T(8,128)(2,1)S(1)} fusion(bf16[128,30,64]{2,0,1:T(8,128)(2,1)S(1)} %bitcast.81, pred[2,32,30,64]{3,2,1,0:T(8,128)(4,1)S(1)} %copy.137, pred[128,64]{1,0:T(8,128)(4,1)S(1)} %and.115), kind=kLoop, calls=%fused_computation.3 | loop fusion | flops 491520 | bytes 1114112 | tf_op jit(solution)/shard_map/jit(_where)/select_n | solution.py:33
  39.6 0.8 %convolution_bitcast_fusion = f32[16,4,2,2,2,16]{5,0,4,3,1,2:T(8,128)S(1)} fusion(bf16[2,8,4,2,64,30,1,1]{4,5,3,2,1,0,7,6:T(8,128)(2,1)S(1)} %bitcast.88, bf16[2,2,16,64,30,1,1,1]{3,2,1,0,4,7,6,5:T(8,128)(2,1)S(1)} %bitcast.96), kind=kOutput, calls=%fused_computation.4 | convolution fusion | flops 31457280 | bytes 770048 | tf_op jit(solution)/shard_map/qki,kxi->qx/dot_general | solution.py:70
  40.6 0.8 %reshape.320 = f32[16,1,512]{2,1,0:T(1,128)} reshape(f32[16,2,2,2,4,16]{5,4,3,2,1,0:T(4,128)S(1)} %bitcast.89) | data formatting | bytes 65536
  41.4 3.7 %all-to-all-start.2 = ((f32[16,1,512]{2,1,0:T(1,128)}), f32[16,1,512]{2,1,0:T(1,128)S(1)}, u32[]{:S(2)}, u32[]{:S(2)}) async-start(f32[16,1,512]{2,1,0:T(1,128)} %reshape.320), calls=%async_computation.2 | async-start | bytes 65536 | tf_op jit(solution)/shard_map/all_to_all | solution.py:77
  45.1 2.5 %fusion.12 = f32[64,30,64]{2,0,1:T(8,128)} fusion(bf16[128,30,64]{2,0,1:T(8,128)(2,1)} %bitcast.82, bf16[128,64]{1,0:T(8,128)(2,1)S(1)} %reshape.306), kind=kOutput, calls=%fused_computation.30 | convolution fusion | flops 31457280 | bytes 999424 | tf_op jit(solution)/shard_map/qki,qx->kxi/dot_general | solution.py:71
  47.5 3.8 %all-to-all-done.2 = f32[16,1,512]{2,1,0:T(1,128)S(1)} async-done(((f32[16,1,512]{2,1,0:T(1,128)}), f32[16,1,512]{2,1,0:T(1,128)S(1)}, u32[]{:S(2)}, u32[]{:S(2)}) %all-to-all-start.2) | async-done | bytes 32800 | tf_op jit(solution)/shard_map/all_to_all | solution.py:77
  51.4 0.5 broadcast.244
  51.9 0.7 %reduce.2 = f32[16,512]{1,0:T(8,128)S(1)} reduce(f32[16,1,512]{2,1,0:T(1,128)S(1)} %all-to-all-done.2, f32[]{:T(128)} %broadcast.244), dimensions={1}, to_apply=%all_to_all.21.reduce_sub_computation | reduce | bytes 65540 | tf_op jit(solution)/shard_map/all_to_all | solution.py:77
  53.3 4.3 %convolution_multiply_fusion = f32[128,3600]{0,1:T(8,128)} fusion(f32[128,64]{0,1:T(8,128)S(1)} %reshape.309, f32[3600,32]{0,1:T(8,128)S(1)} %get-tuple-element.9, f32[3600,32]{0,1:T(8,128)S(1)} %get-tuple-element.8), kind=kOutput, calls=%fused_computation | convolution fusion | flops 354585600 | bytes 2797568 | tf_op jit(solution)/shard_map/dot_general | solution.py:82
  57.6 2.8 %copy.123 = f32[128,3600]{1,0:T(8,128)} copy(f32[128,3600]{0,1:T(8,128)} %convolution_multiply_fusion) | data formatting | bytes 3686400 | tf_op jit(solution)/shard_map/mul | solution.py:82
  (48 shorter events, 3.4 us)
Async XLA Ops:
  0.6 3.0 %copy-start = (f32[2,4,16,3600]{3,2,1,0:T(8,128)S(1)}, f32[2,4,16,3600]{3,2,1,0:T(8,128)}, u32[]{:S(2)}) copy-start(f32[2,4,16,3600]{3,2,1,0:T(8,128)} %param.6) | copy-start | bytes 5529604
  3.7 2.6 %copy-start.4 = (f32[4]{0:T(128)S(1)}, f32[4]{0:T(128)}, u32[]{:S(2)}) copy-start(f32[4]{0:T(128)} %param.7) | copy-start | bytes 52
  3.7 11.2 %copy-start.2 = (s32[2,8,2]{1,2,0:T(2,128)S(1)}, s32[2,8,2]{1,2,0:T(2,128)}, u32[]{:S(2)}) copy-start(s32[2,8,2]{1,2,0:T(2,128)} %param.8) | copy-start | bytes 388
  3.7 11.5 %copy-start.3 = (s32[8,2,8,2]{2,3,1,0:T(2,128)S(1)}, s32[8,2,8,2]{2,3,1,0:T(2,128)}, u32[]{:S(2)}) copy-start(s32[8,2,8,2]{2,3,1,0:T(2,128)} %param.9) | copy-start | bytes 3076
  5.7 10.2 %copy-start.1 = (bf16[1,8,30,4,64]{4,3,2,1,0:T(4,128)(2,1)S(1)}, bf16[1,8,30,4,64]{4,3,2,1,0:T(4,128)(2,1)}, u32[]{:S(2)}) copy-start(bf16[1,8,30,4,64]{4,3,2,1,0:T(4,128)(2,1)} %param.10) | copy-start | bytes 368644
  7.4 13.9 %all-to-all-start = ((bf16[16,2,256]{2,1,0:T(2,128)(2,1)}), bf16[16,2,256]{2,1,0:T(2,128)(2,1)S(1)}, u32[]{:S(2)}, u32[]{:S(2)}) async-start(bf16[16,2,256]{2,1,0:T(2,128)(2,1)} %reshape.318), calls=%async_computation | async-start | bytes 32768 | tf_op jit(solution)/shard_map/all_to_all | solution.py:56
  21.3 11.3 %all-to-all-start.1 = ((bf16[8,2,3840]{2,1,0:T(2,128)(2,1)}), bf16[8,2,3840]{2,1,0:T(2,128)(2,1)}, u32[]{:S(2)}, u32[]{:S(2)}) async-start(bf16[8,2,3840]{2,1,0:T(2,128)(2,1)} %reshape.316), calls=%async_computation.1 | async-start | bytes 245760 | tf_op jit(solution)/shard_map/all_to_all | solution.py:40
  37.8 1.8 %copy-start.5 = (bf16[1,1,30,2,32,64]{5,4,3,2,1,0:T(8,128)(2,1)S(1)}, bf16[1,1,30,2,32,64]{5,4,3,2,1,0:T(8,128)(2,1)}, u32[]{:S(2)}) copy-start(bf16[1,1,30,2,32,64]{5,4,3,2,1,0:T(8,128)(2,1)} %param.11) | copy-start | bytes 737284
  41.4 10.0 %all-to-all-start.2 = ((f32[16,1,512]{2,1,0:T(1,128)}), f32[16,1,512]{2,1,0:T(1,128)S(1)}, u32[]{:S(2)}, u32[]{:S(2)}) async-start(f32[16,1,512]{2,1,0:T(1,128)} %reshape.320), calls=%async_computation.2 | async-start | bytes 65536 | tf_op jit(solution)/shard_map/all_to_all | solution.py:77

commit v2 on v1

v2 whole, which is shorter than its diff:
```python
import functools
import math

import jax
import jax.numpy as jnp
from jax import lax
from jax.experimental import pallas as pl
from jax.experimental.pallas import tpu as pltpu
from jax.sharding import PartitionSpec as P

L = 1800
KB = 64
SHIFT = 6
LANES = 128
WIDE = 512
MESH = pl.DeviceIdType.MESH
ACROSS = (((1,), (1,)), ((), ()))
PLAIN = (((1,), (0,)), ((), ()))


def dot(a, b, dims=PLAIN):
    return lax.dot_general(a, b, dims, preferred_element_type=jnp.float32)


def cosine(phase, length):
    turns = jnp.floor(phase * (1.0 / length) + 0.5)
    angle = (phase - turns * length) * (2.0 * math.pi / length)
    z = angle * angle
    total = jnp.full_like(z, 1.0 / math.factorial(20))
    for n in range(18, -1, -2):
        sign = -1.0 if (n // 2) % 2 else 1.0
        total = total * z + sign / math.factorial(n)
    return total


def split(value):
    high = value.astype(jnp.bfloat16)
    return high, (value - high.astype(jnp.float32)).astype(jnp.bfloat16)


def kernel(
    lat_count,
    spec_count,
    waves_ref,
    skip_ref,
    weight_ref,
    field_ref,
    table_ref,
    given_ref,
    spectrum_ref,
    grid_ref,
    field_buf,
    table_recv,
    stage,
    fold_send,
    fold_recv,
    syn_send,
    syn_recv,
    waves8,
    masked,
    coeffs,
    field_sem,
    table_send_sem,
    table_recv_sem,
    fold_send_sem,
    fold_recv_sem,
    syn_send_sem,
    syn_recv_sem,
):
    f32, bf16 = jnp.float32, jnp.bfloat16
    length = field_ref.shape[1]
    pair_dev = weight_ref.shape[0]
    channels = LANES // (2 * pair_dev)
    slots = given_ref.shape[0]
    columns = given_ref.shape[1]
    dest_count = lat_count * spec_count
    half = 2 * dest_count
    group = 4 * pair_dev
    lat = lax.axis_index("lat")
    spec = lax.axis_index("spec")
    me = spec * lat_count + lat

    def place(t, n, mine):
        return lax.rem(mine + t, n)

    def device(d):
        return {"spec": d // lat_count, "lat": lax.rem(d, lat_count)}

    field_copy = pltpu.make_async_copy(field_ref, field_buf, field_sem)
    field_copy.start()
    barrier = pltpu.get_barrier_semaphore()

    @pl.loop(1, dest_count)
    def _(t):
        pl.semaphore_signal(
            barrier, inc=1, device_id=device(place(t, dest_count, me)), device_id_type=MESH
        )

    pl.semaphore_wait(barrier, dest_count - 1)

    def table_copy(to, slot):
        return pltpu.make_async_remote_copy(
            src_ref=table_ref.at[pl.ds(to * 16, 16)],
            dst_ref=table_recv.at[pl.ds(slot * 16, 16)],
            send_sem=table_send_sem.at[to],
            recv_sem=table_recv_sem.at[slot],
            device_id={"lat": to},
            device_id_type=MESH,
        )

    def fold_copy(to, from_spec, from_lat):
        return pltpu.make_async_remote_copy(
            src_ref=fold_send.at[pl.ds(to * 16, 16)],
            dst_ref=fold_recv.at[from_spec, pl.ds(from_lat * 16, 16)],
            send_sem=fold_send_sem.at[to],
            recv_sem=fold_recv_sem.at[from_spec * lat_count + from_lat],
            device_id=device(to),
            device_id_type=MESH,
        )

    def syn_copy(to, slot):
        return pltpu.make_async_remote_copy(
            src_ref=syn_send.at[pl.ds(lax.rem(to, lat_count) * 16, 16)],
            dst_ref=syn_recv.at[pl.ds(slot * 16, 16)],
            send_sem=syn_send_sem.at[to],
            recv_sem=syn_recv_sem.at[slot],
            device_id=device(to),
            device_id_type=MESH,
        )

    @pl.loop(1, lat_count)
    def _(t):
        table_copy(place(t, lat_count, lat), lat).start()

    own = pl.ds(pl.multiple_of(lat * 16, 16), 16)
    table_recv[own, :] = table_ref[own, :]

    row8 = lax.broadcasted_iota(jnp.int32, (8, LANES), 0)
    tiles = []
    for tile in range(half // 8):
        wave = jnp.zeros((8, LANES), jnp.int32)
        for row in range(8):
            d, s = divmod(tile * 8 + row, 2)
            wave = jnp.where(row8 == row, waves_ref[d // lat_count, s, d % lat_count], wave)
        tiles.append(wave)
    wave = jnp.concatenate(tiles, axis=0).astype(f32)
    lane_half = lax.broadcasted_iota(jnp.int32, (half, LANES), 1).astype(f32)
    fine = wave * lane_half
    coarse = wave * (lane_half * LANES)
    quarter = length // 4
    cos_b, sin_b = cosine(fine, length), cosine(fine - quarter, length)
    cos_a, sin_a = cosine(coarse, length), cosine(coarse - quarter, length)
    base_c = jnp.concatenate([cos_b, -sin_b], axis=0)
    base_s = jnp.concatenate([sin_b, cos_b], axis=0)
    turn_c = jnp.concatenate([cos_a, cos_a], axis=0)
    turn_s = jnp.concatenate([sin_a, sin_a], axis=0)
    full = length // LANES
    for a in range(pl.cdiv(length, LANES)):
        width = min(LANES, length - a * LANES)
        part = turn_c[:, a : a + 1] * base_c - turn_s[:, a : a + 1] * base_s
        high, low = split(part)
        waves8[0 : 2 * half, a * LANES : a * LANES + width] = high[:, :width]
        waves8[2 * half : 4 * half, a * LANES : a * LANES + width] = low[:, :width]

    for pair in range(slots // 2):
        both = jnp.concatenate([given_ref[2 * pair], given_ref[2 * pair + 1]], axis=1)
        coeffs[0:columns, pair * LANES : (pair + 1) * LANES] = both
        coeffs[columns : 2 * columns, pair * LANES : (pair + 1) * LANES] = both
    rest = coeffs.shape[1] - slots * KB
    coeffs[:, slots * KB :] = jnp.zeros((2 * columns, rest), bf16)

    field_copy.wait()
    cuts = list(range(0, full * LANES, WIDE)) + [full * LANES]
    cuts = [(b, min(b + WIDE, full * LANES)) for b in cuts[:-1]] + (
        [(full * LANES, length)] if full * LANES < length else []
    )
    total = jnp.zeros((4 * half, LANES), f32)
    for begin, end in cuts:
        high, low = split(field_buf[:, begin:end])
        part = waves8[:, begin:end]
        total = total + dot(part, high, ACROSS) + dot(part, low, ACROSS)
    fourier = total[: 2 * half] + total[2 * half :]

    lane = lax.broadcasted_iota(jnp.int32, (half, LANES), 1)
    pair_of = (lane // channels) % pair_dev
    weight = jnp.zeros((half, LANES), f32)
    for j in range(pair_dev):
        weight = jnp.where(pair_of == j, weight_ref[j], weight)
    weight = weight * (1.0 / length)

    def butterfly(value):
        turned = pltpu.roll(value, LANES // 2, 1)
        return (turned + jnp.where(lane < LANES // 2, value, -value)) * weight

    folded = [butterfly(fourier[:half]), butterfly(fourier[half:])]
    offsets = [r * spec_count * channels + spec * channels for r in range(2)]
    for pj in range(2 * pair_dev):
        placed = jnp.zeros((half, LANES), f32)
        for r in range(2):
            turned = pltpu.roll(
                folded[r], lax.rem(offsets[r] + (LANES - pj * channels), LANES), 1
            )
            here = (lane >= offsets[r]) & (lane < offsets[r] + channels)
            placed = jnp.where(here, turned, placed)
        stage[pl.ds(pj, half, stride=2 * pair_dev), :] = placed
    fold_send[...] = stage[...].astype(bf16)

    @pl.loop(1, dest_count)
    def _(t):
        fold_copy(place(t, dest_count, me), spec, lat).start()

    mine = pl.ds(pl.multiple_of(me * 16, 16), 16)
    fold_recv[spec, own, :] = fold_send[mine, :]

    m0, m1 = waves_ref[spec, 0, lat], waves_ref[spec, 1, lat]
    start1 = KB * ((L + KB - m0) >> SHIFT)
    lows, highs = [], []
    for b in range(lat_count):
        for s, (m, start) in enumerate(((m0, 0), (m1, start1))):
            lows.append(jnp.full((2 * pair_dev, LANES), start + KB * skip_ref[b, spec, s, lat]))
            highs.append(jnp.full((2 * pair_dev, LANES), L - m + start))
    lowest = jnp.concatenate(lows, axis=0)
    highest = jnp.concatenate(highs, axis=0)
    rows = lat_count * group
    row_q = lax.broadcasted_iota(jnp.int32, (rows, LANES), 0)
    lane_q = lax.broadcasted_iota(jnp.int32, (rows, LANES), 1)
    parity_ok = (lane_q & 1) == ((row_q // pair_dev) & 1)
    pick_row = lax.broadcasted_iota(jnp.int32, (rows, lat_count * 16), 0)
    pick_col = lax.broadcasted_iota(jnp.int32, (rows, lat_count * 16), 1)
    same_band = (pick_row // group) == (pick_col // 16)

    @pl.loop(1, lat_count)
    def _(t):
        table_copy(lat, place(t, lat_count, lat)).wait_recv()

    blocks = table_recv[...]
    for u in range(masked.shape[1] // WIDE):
        chosen = same_band & ((pick_col % 16) == u * pair_dev + pick_row % pair_dev)
        pick = jnp.where(chosen, 1.0, 0.0).astype(bf16)
        spread = dot(pick, blocks)
        for v in range(WIDE // LANES):
            at = u * WIDE + v * LANES
            spot = lane_q + at
            keep = parity_ok & (spot >= lowest) & (spot <= highest)
            piece = spread[:, v * LANES : (v + 1) * LANES]
            masked[:, at : at + LANES] = jnp.where(keep, piece, 0.0).astype(bf16)

    synthesis = dot(masked[...], coeffs[...], ACROSS)
    rounded = synthesis.astype(bf16).astype(f32)
    syn_send[...] = jnp.where(lane_q < columns, rounded, synthesis - rounded).astype(bf16)

    @pl.loop(1, dest_count)
    def _(t):
        syn_copy(place(t, dest_count, me), me).start()

    syn_recv[mine, :] = syn_send[own, :]

    @pl.loop(1, dest_count)
    def _(t):
        d = place(t, dest_count, me)
        fold_copy(me, d // lat_count, lax.rem(d, lat_count)).wait_recv()

    gathered = fold_recv[0].astype(f32)
    for q in range(1, spec_count):
        gathered = gathered + fold_recv[q].astype(f32)
    folded_own = gathered.T[:columns].astype(bf16)
    for u in range(masked.shape[1] // WIDE):
        part = dot(folded_own, masked[:, u * WIDE : (u + 1) * WIDE])
        for k in range(u * WIDE // KB, min((u + 1) * WIDE // KB, slots)):
            at = k * KB - u * WIDE
            spectrum_ref[k] = part[:, at : at + KB]

    @pl.loop(1, dest_count)
    def _(t):
        syn_copy(me, place(t, dest_count, me)).wait_recv()

    received = syn_recv[...].astype(f32)
    stage[...] = received + pltpu.roll(received, LANES // 2, 1)
    back = [jnp.zeros((half, LANES), f32) for _ in range(2)]
    for pj in range(2 * pair_dev):
        value = stage[pl.ds(pj, half, stride=2 * pair_dev), :]
        for r in range(2):
            turned = pltpu.roll(value, lax.rem(LANES + pj * channels - offsets[r], LANES), 1)
            back[r] = jnp.where((lane // channels) == pj, turned, back[r])
    back = jnp.concatenate([butterfly(back[0]), butterfly(back[1])], axis=0)
    high, low = split(jnp.concatenate([back, back], axis=0).T)
    for begin, end in cuts:
        part = waves8[:, begin:end]
        grid_ref[:, begin:end] = dot(high, part) + dot(low, part)

    @pl.loop(1, lat_count)
    def _(t):
        table_copy(place(t, lat_count, lat), lat).wait_send()

    @pl.loop(1, dest_count)
    def _(t):
        d = place(t, dest_count, me)
        fold_copy(d, spec, lat).wait_send()
        syn_copy(d, me).wait_send()


def on_device(
    lat_count, spec_count, field_grid, quad_weight, owner_waves, skip_blocks, legendre_table, given_spectrum
):
    hemispheres, pair_dev, channels, length = field_grid.shape
    slots = given_spectrum.shape[2]
    columns = 2 * given_spectrum.shape[4]
    dest_count = lat_count * spec_count
    rows = lat_count * 4 * pair_dev
    per_wide = WIDE // KB
    quarters = 16 // pair_dev
    table = legendre_table[0]
    table = jnp.pad(table, ((0, 0), (0, quarters * per_wide - slots), (0, 0), (0, 0)))
    table = table.reshape(lat_count, quarters, per_wide, pair_dev, KB)
    table = jnp.transpose(table, (0, 1, 3, 2, 4)).reshape(lat_count * 16, WIDE)
    half = 2 * dest_count
    f32, bf16 = jnp.float32, jnp.bfloat16
    vmem = pl.BlockSpec(memory_space=pltpu.VMEM)
    smem = pl.BlockSpec(memory_space=pltpu.SMEM)
    dma = pltpu.SemaphoreType.DMA
    spectrum, back_grid = pl.pallas_call(
        functools.partial(kernel, lat_count, spec_count),
        out_shape=(
            jax.ShapeDtypeStruct((slots, columns, KB), f32),
            jax.ShapeDtypeStruct((LANES, length), f32),
        ),
        in_specs=[smem, smem, smem, pl.BlockSpec(memory_space=pl.ANY), vmem, vmem],
        out_specs=(vmem, vmem),
        scratch_shapes=[
            pltpu.VMEM((LANES, length), f32),
            pltpu.VMEM((lat_count * 16, WIDE), bf16),
            pltpu.VMEM((dest_count * 16, LANES), f32),
            pltpu.VMEM((dest_count * 16, LANES), bf16),
            pltpu.VMEM((spec_count, rows, LANES), bf16),
            pltpu.VMEM((rows, LANES), bf16),
            pltpu.VMEM((dest_count * 16, LANES), bf16),
            pltpu.VMEM((4 * half, length), bf16),
            pltpu.VMEM((rows, quarters * WIDE), bf16),
            pltpu.VMEM((2 * columns, quarters * WIDE), bf16),
            dma,
            dma((lat_count,)),
            dma((lat_count,)),
            dma((dest_count,)),
            dma((dest_count,)),
            dma((dest_count,)),
            dma((dest_count,)),
        ],
        compiler_params=pltpu.CompilerParams(
            collective_id=0, has_side_effects=True, vmem_limit_bytes=48 * 2**20
        ),
        name="transform",
    )(
        jnp.transpose(owner_waves, (0, 2, 1)),
        jnp.transpose(skip_blocks, (0, 1, 3, 2)),
        quad_weight,
        field_grid.reshape(LANES, length),
        table,
        given_spectrum.reshape(slots, columns, KB),
    )
    return (spectrum.reshape(given_spectrum.shape), back_grid.reshape(field_grid.shape))


def solution(mesh):
    lat_count, spec_count = mesh.shape["lat"], mesh.shape["spec"]

    def body(*args):
        return on_device(lat_count, spec_count, *args)

    return jax.shard_map(
        body,
        mesh=mesh,
        in_specs=(
            P(None, "lat", ("group", "spec"), None),
            P("lat"),
            P(),
            P(),
            P("spec", None, None, "lat", None),
            P("spec", "lat", None, None, "group", None),
        ),
        out_specs=(
            P("spec", "lat", None, None, "group", None),
            P(None, "lat", ("group", "spec"), None),
        ),
        check_vma=False,
    )
```

time: 60.9 us -> 28.8 us (0.47)
  Pallas kernels: 0 us -> 19.7 us
  starting transfers between devices: 15 us -> 0 us
  waiting for transfers between devices: 14.7 us -> 0 us
  matrix products: 9.59 us -> 0 us
  other arithmetic: 7.02 us -> 0 us
  local copies, waits for them, and re-layouts: 13 us -> 8.13 us
    pallas_call x0 -> x1, Pallas kernels: none -> 19.7 us  [on_device(): pl.pallas_call(functools.partial(kernel, lat_count, spec_count), out_shap...]
    all_to_all x3 -> x0, starting transfers between devices: 15 us -> none  [the longest x1 7.39 us: on_device(): lax.all_to_all(folded, ('spec', 'lat'), split_axis=0, concat_axis=0, tile...]
    all_to_all x3 -> x0, waiting for transfers between devices: 14.7 us -> none  [the longest x1 6.36 us: on_device(): lax.all_to_all(legendre_table[0], 'lat', split_axis=0, concat_axis=2, til...]
    dot_general x4 -> x0, matrix products: 9.59 us -> none  [the longest x1 4.35 us: on_device(): jnp.dot(back, wave_table.T, precision=lax.Precision.HIGHEST, preferred_el...]
    select_n x4 -> x0, other arithmetic: 3.22 us -> none  [the longest x2 3.2 us: owner_table(): return jnp.where(keep, moved, jnp.zeros((), blocks.dtype))]
    mul x2 -> x0, local copies, waits for them, and re-layouts: 2.89 us -> none  [the longest x1 2.81 us: on_device(): jnp.dot(back, wave_table.T, precision=lax.Precision.HIGHEST, preferred_el...]
    cos x1 -> x0, other arithmetic: 2 us -> none  [fourier_table(): return jnp.concatenate([jnp.cos(angles), -jnp.sin(angles)], axis=1)]
    all_to_all x3 -> x0, local copies, waits for them, and re-layouts: 1.59 us -> none  [the longest x1 1.03 us: on_device(): lax.all_to_all(legendre_table[0], 'lat', split_axis=0, concat_axis=2, til...]
  transfers between devices with their start and end apart: 3 -> 0, of which waited for: 3 -> 0; matrix products, arithmetic and copies ran while one was open for 9% -> 0% of each run, Pallas kernels for 0% -> 0%
where the time goes in v2:
time: 28.8 us; the launch traced here: 28.5 us
  Pallas kernels  19.7 us (68%)
  local copies, waits for them, and re-layouts  8.13 us (28%)
  between operations  0.66 us (2%)
    pallas_call x1, Pallas kernels, on_device(): pl.pallas_call(functools.partial(kernel, lat_count, spec_count), out_shap...  19.7 us
    unnamed x12, local copies, waits for them, and re-layouts  6.8 us
    pad x1, local copies, waits for them, and re-layouts, on_device(): jnp.pad(table, ((0, 0), (0, quarters * per_wide - slots), (0, 0), (0, 0)))  1.08 us

profile of v2, /device:TPU:0, one launch (start us, length us, event | category | flops | bytes accessed | tf_op | source)
XLA Modules:
  0.0 28.5 jit_solution(13647313650292650833)
XLA Ops:
  0.6 1.1 %pad.4 = bf16[8,32,4,64]{3,2,1,0:T(4,128)(2,1)S(1)} pad(bf16[8,30,4,64]{3,2,1,0:T(4,128)(2,1)} %bitcast.21, bf16[]{:T(256)} %constant.2.clone.1), padding=0_0x0_2x0_0x0_0 | pad | bytes 253954 | tf_op jit(solution)/shard_map/jit(_pad)/pad | solution.py:313
  1.8 0.2 reshape.24.table_ref
  2.0 0.0 copy-start
  2.0 1.5 %copy-done = f32[2,4,16,3600]{3,2,1,0:T(8,128)S(1)} copy-done((f32[2,4,16,3600]{3,2,1,0:T(8,128)S(1)}, f32[2,4,16,3600]{3,2,1,0:T(8,128)}, u32[]{:S(2)}) %copy-start) | copy-done | bytes 1843224
  3.5 0.0 copy-start.1
  3.5 1.0 %copy-done.1 = bf16[1,1,30,2,32,64]{5,4,3,2,1,0:T(8,128)(2,1)S(1)} copy-done((bf16[1,1,30,2,32,64]{5,4,3,2,1,0:T(8,128)(2,1)S(1)}, bf16[1,1,30,2,32,64]{5,4,3,2,1,0:T(8,128)(2,1)}, u32[]{:S(2)}) %copy-start.1) | copy-done | bytes 245784
  4.5 0.0 copy-start.2
  4.5 0.7 %copy-done.2 = s32[8,2,8,2]{2,3,1,0:T(2,128)S(1)} copy-done((s32[8,2,8,2]{2,3,1,0:T(2,128)S(1)}, s32[8,2,8,2]{2,3,1,0:T(2,128)}, u32[]{:S(2)}) %copy-start.2) | copy-done | bytes 1048
  5.2 0.0 copy-start.3
  5.2 0.7 %copy-done.3 = s32[2,8,2]{1,2,0:T(2,128)S(1)} copy-done((s32[2,8,2]{1,2,0:T(2,128)S(1)}, s32[2,8,2]{1,2,0:T(2,128)}, u32[]{:S(2)}) %copy-start.3) | copy-done | bytes 152
  5.9 0.0 copy-start.4
  5.9 0.7 %copy-done.4 = f32[4]{0:T(128)S(1)} copy-done((f32[4]{0:T(128)S(1)}, f32[4]{0:T(128)}, u32[]{:S(2)}) %copy-start.4) | copy-done | bytes 40
  6.6 19.7 %transform.1 = (f32[30,64,64]{2,1,0:T(8,128)S(1)}, f32[128,3600]{1,0:T(8,128)S(1)}) custom-call(s32[2,2,8]{2,1,0:T(2,128)S(1)} %bitcast.18, s32[8,2,2,8]{3,2,1,0:T(2,128)S(1)} %bitcast.17, f32[4]{0:T(128)S(1)} %copy-done.4, f32[128,3600]{1,0:T(8,128)S(1)} %bitcast.13, bf16[128,512]{1,0:T(8,128)(2,1)S(1)} %reshape.24.table_ref, bf16[30,64,64]{2,1,0:T(8,128)(2,1)S(1)} %bitcast.16), custom_call_target="tpu_custom_call" | custom-call | tf_op jit(solution)/shard_map/transform/pallas_call | solution.py:321
  26.3 0.9 %copy.13 = f32[1,1,30,2,32,64]{5,4,3,2,1,0:T(8,128)} copy(f32[1,1,30,2,32,64]{5,4,3,2,1,0:T(8,128)S(1)} %bitcast.15) | data formatting | bytes 983040
  27.2 1.2 %copy.14 = f32[2,4,16,3600]{3,2,1,0:T(8,128)} copy(f32[2,4,16,3600]{3,2,1,0:T(8,128)S(1)} %bitcast.14) | data formatting | bytes 3686400
  (1 shorter events, 0.0 us)
Async XLA Ops:
  2.0 1.5 %copy-start = (f32[2,4,16,3600]{3,2,1,0:T(8,128)S(1)}, f32[2,4,16,3600]{3,2,1,0:T(8,128)}, u32[]{:S(2)}) copy-start(f32[2,4,16,3600]{3,2,1,0:T(8,128)} %param.6) | copy-start | bytes 5529604
  3.5 1.0 %copy-start.1 = (bf16[1,1,30,2,32,64]{5,4,3,2,1,0:T(8,128)(2,1)S(1)}, bf16[1,1,30,2,32,64]{5,4,3,2,1,0:T(8,128)(2,1)}, u32[]{:S(2)}) copy-start(bf16[1,1,30,2,32,64]{5,4,3,2,1,0:T(8,128)(2,1)} %param.11) | copy-start | bytes 737284
  4.5 0.7 %copy-start.2 = (s32[8,2,8,2]{2,3,1,0:T(2,128)S(1)}, s32[8,2,8,2]{2,3,1,0:T(2,128)}, u32[]{:S(2)}) copy-start(s32[8,2,8,2]{2,3,1,0:T(2,128)} %param.9) | copy-start | bytes 3076
  5.2 0.7 %copy-start.3 = (s32[2,8,2]{1,2,0:T(2,128)S(1)}, s32[2,8,2]{1,2,0:T(2,128)}, u32[]{:S(2)}) copy-start(s32[2,8,2]{1,2,0:T(2,128)} %param.8) | copy-start | bytes 388
  5.9 0.7 %copy-start.4 = (f32[4]{0:T(128)S(1)}, f32[4]{0:T(128)}, u32[]{:S(2)}) copy-start(f32[4]{0:T(128)} %weight_ref.1) | copy-start | bytes 52

commit v3 on v2

--- a/solution.py
+++ b/solution.py
@@ -41,14 +41,21 @@
 def kernel(
     lat_count,
     spec_count,
+    waves_hbm,
+    skip_hbm,
+    weight_hbm,
+    field_ref,
+    table_ref,
+    given_hbm,
+    spectrum_ref,
+    grid_ref,
+    rest_ref,
+    high_ref,
+    low_ref,
     waves_ref,
     skip_ref,
     weight_ref,
-    field_ref,
-    table_ref,
     given_ref,
-    spectrum_ref,
-    grid_ref,
     field_buf,
     table_recv,
     stage,
@@ -59,7 +66,7 @@
     waves8,
     masked,
     coeffs,
-    field_sem,
+    local_sem,
     table_send_sem,
     table_recv_sem,
     fold_send_sem,
@@ -86,8 +93,13 @@
     def device(d):
         return {"spec": d // lat_count, "lat": lax.rem(d, lat_count)}
 
-    field_copy = pltpu.make_async_copy(field_ref, field_buf, field_sem)
-    field_copy.start()
+    waves_copy = pltpu.make_async_copy(waves_hbm, waves_ref, local_sem.at[0])
+    skip_copy = pltpu.make_async_copy(skip_hbm, skip_ref, local_sem.at[1])
+    weight_copy = pltpu.make_async_copy(weight_hbm, weight_ref, local_sem.at[2])
+    given_copy = pltpu.make_async_copy(given_hbm, given_ref, local_sem.at[3])
+    field_copy = pltpu.make_async_copy(field_ref, field_buf, local_sem.at[4])
+    for copy in (waves_copy, skip_copy, weight_copy, given_copy, field_copy):
+        copy.start()
     barrier = pltpu.get_barrier_semaphore()
 
     @pl.loop(1, dest_count)
@@ -133,7 +145,11 @@
         table_copy(place(t, lat_count, lat), lat).start()
 
     own = pl.ds(pl.multiple_of(lat * 16, 16), 16)
+    mine = pl.ds(pl.multiple_of(me * 16, 16), 16)
     table_recv[own, :] = table_ref[own, :]
+
+    for copy in (waves_copy, skip_copy, weight_copy):
+        copy.wait()
 
     row8 = lax.broadcasted_iota(jnp.int32, (8, LANES), 0)
     tiles = []
@@ -162,55 +178,13 @@
         waves8[0 : 2 * half, a * LANES : a * LANES + width] = high[:, :width]
         waves8[2 * half : 4 * half, a * LANES : a * LANES + width] = low[:, :width]
 
+    given_copy.wait()
     for pair in range(slots // 2):
         both = jnp.concatenate([given_ref[2 * pair], given_ref[2 * pair + 1]], axis=1)
         coeffs[0:columns, pair * LANES : (pair + 1) * LANES] = both
         coeffs[columns : 2 * columns, pair * LANES : (pair + 1) * LANES] = both
     rest = coeffs.shape[1] - slots * KB
     coeffs[:, slots * KB :] = jnp.zeros((2 * columns, rest), bf16)
-
-    field_copy.wait()
-    cuts = list(range(0, full * LANES, WIDE)) + [full * LANES]
-    cuts = [(b, min(b + WIDE, full * LANES)) for b in cuts[:-1]] + (
-        [(full * LANES, length)] if full * LANES < length else []
-    )
-    total = jnp.zeros((4 * half, LANES), f32)
-    for begin, end in cuts:
-        high, low = split(field_buf[:, begin:end])
-        part = waves8[:, begin:end]
-        total = total + dot(part, high, ACROSS) + dot(part, low, ACROSS)
-    fourier = total[: 2 * half] + total[2 * half :]
-
-    lane = lax.broadcasted_iota(jnp.int32, (half, LANES), 1)
-    pair_of = (lane // channels) % pair_dev
-    weight = jnp.zeros((half, LANES), f32)
-    for j in range(pair_dev):
-        weight = jnp.where(pair_of == j, weight_ref[j], weight)
-    weight = weight * (1.0 / length)
-
-    def butterfly(value):
-        turned = pltpu.roll(value, LANES // 2, 1)
-        return (turned + jnp.where(lane < LANES // 2, value, -value)) * weight
-
-    folded = [butterfly(fourier[:half]), butterfly(fourier[half:])]
-    offsets = [r * spec_count * channels + spec * channels for r in range(2)]
-    for pj in range(2 * pair_dev):
-        placed = jnp.zeros((half, LANES), f32)
-        for r in range(2):
-            turned = pltpu.roll(
-                folded[r], lax.rem(offsets[r] + (LANES - pj * channels), LANES), 1
-            )
-            here = (lane >= offsets[r]) & (lane < offsets[r] + channels)
-            placed = jnp.where(here, turned, placed)
-        stage[pl.ds(pj, half, stride=2 * pair_dev), :] = placed
-    fold_send[...] = stage[...].astype(bf16)
-
-    @pl.loop(1, dest_count)
-    def _(t):
-        fold_copy(place(t, dest_count, me), spec, lat).start()
-
-    mine = pl.ds(pl.multiple_of(me * 16, 16), 16)
-    fold_recv[spec, own, :] = fold_send[mine, :]
 
     m0, m1 = waves_ref[spec, 0, lat], waves_ref[spec, 1, lat]
     start1 = KB * ((L + KB - m0) >> SHIFT)
@@ -255,20 +229,47 @@
 
     syn_recv[mine, :] = syn_send[own, :]
 
-    @pl.loop(1, dest_count)
-    def _(t):
-        d = place(t, dest_count, me)
-        fold_copy(me, d // lat_count, lax.rem(d, lat_count)).wait_recv()
-
-    gathered = fold_recv[0].astype(f32)
-    for q in range(1, spec_count):
-        gathered = gathered + fold_recv[q].astype(f32)
-    folded_own = gathered.T[:columns].astype(bf16)
-    for u in range(masked.shape[1] // WIDE):
-        part = dot(folded_own, masked[:, u * WIDE : (u + 1) * WIDE])
-        for k in range(u * WIDE // KB, min((u + 1) * WIDE // KB, slots)):
-            at = k * KB - u * WIDE
-            spectrum_ref[k] = part[:, at : at + KB]
+    field_copy.wait()
+    cuts = list(range(0, full * LANES, WIDE)) + [full * LANES]
+    cuts = [(b, min(b + WIDE, full * LANES)) for b in cuts[:-1]] + (
+        [(full * LANES, length)] if full * LANES < length else []
+    )
+    total = jnp.zeros((4 * half, LANES), f32)
+    for begin, end in cuts:
+        high, low = split(field_buf[:, begin:end])
+        part = waves8[:, begin:end]
+        total = total + dot(part, high, ACROSS) + dot(part, low, ACROSS)
+    fourier = total[: 2 * half] + total[2 * half :]
+
+    lane = lax.broadcasted_iota(jnp.int32, (half, LANES), 1)
+    pair_of = (lane // channels) % pair_dev
+    weight = jnp.zeros((half, LANES), f32)
+    for j in range(pair_dev):
+        weight = jnp.where(pair_of == j, weight_ref[j], weight)
+    weight = weight * (1.0 / length)
+
+    def butterfly(value):
+        turned = pltpu.roll(value, LANES // 2, 1)
+        return (turned + jnp.where(lane < LANES // 2, value, -value)) * weight
+
+    folded = [butterfly(fourier[:half]), butterfly(fourier[half:])]
+    offsets = [r * spec_count * channels + spec * channels for r in range(2)]
+    for pj in range(2 * pair_dev):
+        placed = jnp.zeros((half, LANES), f32)
+        for r in range(2):
+            turned = pltpu.roll(
+                folded[r], lax.rem(offsets[r] + (LANES - pj * channels), LANES), 1
+            )
+            here = (lane >= offsets[r]) & (lane < offsets[r] + channels)
+            placed = jnp.where(here, turned, placed)
+        stage[pl.ds(pj, half, stride=2 * pair_dev), :] = placed
+    fold_send[...] = stage[...].astype(bf16)
+
+    @pl.loop(1, dest_count)
+    def _(t):
+        fold_copy(place(t, dest_count, me), spec, lat).start()
+
+    fold_recv[spec, own, :] = fold_send[mine, :]
 
     @pl.loop(1, dest_count)
     def _(t):
@@ -284,9 +285,29 @@
             back[r] = jnp.where((lane // channels) == pj, turned, back[r])
     back = jnp.concatenate([butterfly(back[0]), butterfly(back[1])], axis=0)
     high, low = split(jnp.concatenate([back, back], axis=0).T)
+    high_ref[...] = high
+    low_ref[...] = low
+    done = grid_ref.shape[1]
     for begin, end in cuts:
-        part = waves8[:, begin:end]
-        grid_ref[:, begin:end] = dot(high, part) + dot(low, part)
+        if end <= done:
+            part = waves8[:, begin:end]
+            grid_ref[:, begin:end] = dot(high, part) + dot(low, part)
+    rest_ref[...] = waves8[:, done:]
+
+    @pl.loop(1, dest_count)
+    def _(t):
+        d = place(t, dest_count, me)
+        fold_copy(me, d // lat_count, lax.rem(d, lat_count)).wait_recv()
+
+    gathered = fold_recv[0].astype(f32)
+    for q in range(1, spec_count):
+        gathered = gathered + fold_recv[q].astype(f32)
+    folded_own = gathered.T[:columns].astype(bf16)
+    for u in range(masked.shape[1] // WIDE):
+        part = dot(folded_own, masked[:, u * WIDE : (u + 1) * WIDE])
+        for k in range(u * WIDE // KB, min((u + 1) * WIDE // KB, slots)):
+            at = k * KB - u * WIDE
+            spectrum_ref[k] = part[:, at : at + KB]
 
     @pl.loop(1, lat_count)
     def _(t):
@@ -297,6 +318,35 @@
         d = place(t, dest_count, me)
         fold_copy(d, spec, lat).wait_send()
         syn_copy(d, me).wait_send()
+
+
+def write_kernel(spectrum_in, grid_in, rest_ref, high_ref, low_ref, spectrum_ref, grid_ref, buf, sem):
+    done = grid_in.shape[1]
+    length = grid_ref.shape[1]
+    copies = [
+        pltpu.make_async_copy(grid_in, grid_ref.at[:, pl.ds(0, done)], sem.at[0]),
+        pltpu.make_async_copy(spectrum_in, spectrum_ref, sem.at[1]),
+    ]
+    for copy in copies:
+        copy.start()
+    high, low = high_ref[...], low_ref[...]
+    for n, begin in enumerate(range(0, length - done, WIDE)):
+        end = min(begin + WIDE, length - done)
+        if length - done - end < LANES:
+            end = length - done
+        if begin >= end or n >= sem.shape[0] - 2:
+            break
+        part = rest_ref[:, begin:end]
+        buf[:, begin:end] = dot(high, part) + dot(low, part)
+        copy = pltpu.make_async_copy(
+            buf.at[:, pl.ds(begin, end - begin)],
+            grid_ref.at[:, pl.ds(done + begin, end - begin)],
+            sem.at[2 + n],
+        )
+        copy.start()
+        copies.append(copy)
+    for copy in copies:
+        copy.wait()
 
 
 def on_device(
@@ -318,15 +368,27 @@
     vmem = pl.BlockSpec(memory_space=pltpu.VMEM)
     smem = pl.BlockSpec(memory_space=pltpu.SMEM)
     dma = pltpu.SemaphoreType.DMA
-    spectrum, back_grid = pl.pallas_call(
+    hbm = pl.BlockSpec(memory_space=pltpu.HBM)
+    done = (length // 2) // WIDE * WIDE + WIDE
+    rest = length - done
+    parts = rest // WIDE + (1 if rest % WIDE >= LANES else 0)
+    stack = jax.ShapeDtypeStruct((LANES, 4 * half), bf16)
+    spectrum, first, waves_rest, high, low = pl.pallas_call(
         functools.partial(kernel, lat_count, spec_count),
         out_shape=(
             jax.ShapeDtypeStruct((slots, columns, KB), f32),
-            jax.ShapeDtypeStruct((LANES, length), f32),
+            jax.ShapeDtypeStruct((LANES, done), f32),
+            jax.ShapeDtypeStruct((4 * half, rest), bf16),
+            stack,
+            stack,
         ),
-        in_specs=[smem, smem, smem, pl.BlockSpec(memory_space=pl.ANY), vmem, vmem],
-        out_specs=(vmem, vmem),
+        in_specs=[hbm, hbm, hbm, hbm, vmem, hbm],
+        out_specs=(vmem,) * 5,
         scratch_shapes=[
+            pltpu.SMEM((spec_count, 2, lat_count), jnp.int32),
+            pltpu.SMEM((lat_count, spec_count, 2, lat_count), jnp.int32),
+            pltpu.SMEM((pair_dev,), f32),
+            pltpu.VMEM((slots, columns, KB), bf16),
             pltpu.VMEM((LANES, length), f32),
             pltpu.VMEM((lat_count * 16, WIDE), bf16),
             pltpu.VMEM((dest_count * 16, LANES), f32),
@@ -337,7 +399,7 @@
             pltpu.VMEM((4 * half, length), bf16),
             pltpu.VMEM((rows, quarters * WIDE), bf16),
             pltpu.VMEM((2 * columns, quarters * WIDE), bf16),
-            dma,
+            dma((5,)),
             dma((lat_count,)),
             dma((lat_count,)),
             dma((dest_count,)),
@@ -346,7 +408,7 @@
             dma((dest_count,)),
         ],
         compiler_params=pltpu.CompilerParams(
-            collective_id=0, has_side_effects=True, vmem_limit_bytes=48 * 2**20
+            collective_id=0, has_side_effects=True, vmem_limit_bytes=32 * 2**20
         ),
         name="transform",
     )(
@@ -357,6 +419,18 @@
         table,
         given_spectrum.reshape(slots, columns, KB),
     )
+    spectrum, back_grid = pl.pallas_call(
+        write_kernel,
+        out_shape=(
+            jax.ShapeDtypeStruct((slots, columns, KB), f32),
+            jax.ShapeDtypeStruct((LANES, length), f32),
+        ),
+        in_specs=[vmem] * 5,
+        out_specs=(hbm, hbm),
+        scratch_shapes=[pltpu.VMEM((LANES, rest), f32), dma((2 + parts,))],
+        compiler_params=pltpu.CompilerParams(vmem_limit_bytes=16 * 2**20),
+        name="write_out",
+    )(spectrum, first, waves_rest, high, low)
     return (spectrum.reshape(given_spectrum.shape), back_grid.reshape(field_grid.shape))
 
 

time: 28.8 us -> 28.4 us (0.986)
  local copies, waits for them, and re-layouts: 8.13 us -> 5.93 us
  Pallas kernels: 19.7 us -> 21.5 us
    unnamed x12 -> x10, local copies, waits for them, and re-layouts: 6.8 us -> 4.6 us
    pallas_call x0 -> x1, Pallas kernels: none -> 1.62 us  [on_device(): pl.pallas_call(write_kernel, out_shape=(jax.ShapeDtypeStruct((slots, colu...]
where the time goes in v3:
time: 28.4 us; the launch traced here: 28.1 us
  Pallas kernels  21.5 us (76%)
  local copies, waits for them, and re-layouts  5.93 us (21%)
  between operations  0.66 us (2%)
    pallas_call x1, Pallas kernels, on_device(): pl.pallas_call(functools.partial(kernel, lat_count, spec_count), out_shap...  19.9 us
    unnamed x10, local copies, waits for them, and re-layouts  4.6 us
    pallas_call x1, Pallas kernels, on_device(): pl.pallas_call(write_kernel, out_shape=(jax.ShapeDtypeStruct((slots, colu...  1.62 us
    pad x1, local copies, waits for them, and re-layouts, on_device(): jnp.pad(table, ((0, 0), (0, quarters * per_wide - slots), (0, 0), (0, 0)))  1.08 us

profile of v3, /device:TPU:0, one launch (start us, length us, event | category | flops | bytes accessed | tf_op | source)
XLA Modules:
  0.0 28.1 jit_solution(4184525289859358703)
XLA Ops:
  0.6 1.1 %pad.4 = bf16[8,32,4,64]{3,2,1,0:T(4,128)(2,1)S(1)} pad(bf16[8,30,4,64]{3,2,1,0:T(4,128)(2,1)} %bitcast.19, bf16[]{:T(256)} %constant.2.clone.1), padding=0_0x0_2x0_0x0_0 | pad | bytes 253954 | tf_op jit(solution)/shard_map/jit(_pad)/pad | solution.py:363
  1.8 0.2 reshape.24.table_ref
  2.0 0.0 copy-start
  2.0 1.5 %copy-done = f32[2,4,16,3600]{3,2,1,0:T(8,128)S(1)} copy-done((f32[2,4,16,3600]{3,2,1,0:T(8,128)S(1)}, f32[2,4,16,3600]{3,2,1,0:T(8,128)}, u32[]{:S(2)}) %copy-start) | copy-done | bytes 1843224
  3.5 0.0 copy-start.1
  3.5 1.0 %copy-done.1 = bf16[1,1,30,2,32,64]{5,4,3,2,1,0:T(8,128)(2,1)S(1)} copy-done((bf16[1,1,30,2,32,64]{5,4,3,2,1,0:T(8,128)(2,1)S(1)}, bf16[1,1,30,2,32,64]{5,4,3,2,1,0:T(8,128)(2,1)}, u32[]{:S(2)}) %copy-start.1) | copy-done | bytes 245784
  4.5 0.0 copy-start.2
  4.5 0.7 %copy-done.2 = s32[8,2,8,2]{2,3,1,0:T(2,128)S(1)} copy-done((s32[8,2,8,2]{2,3,1,0:T(2,128)S(1)}, s32[8,2,8,2]{2,3,1,0:T(2,128)}, u32[]{:S(2)}) %copy-start.2) | copy-done | bytes 1048
  5.2 0.0 copy-start.3
  5.2 0.7 %copy-done.3 = s32[2,8,2]{1,2,0:T(2,128)S(1)} copy-done((s32[2,8,2]{1,2,0:T(2,128)S(1)}, s32[2,8,2]{1,2,0:T(2,128)}, u32[]{:S(2)}) %copy-start.3) | copy-done | bytes 152
  5.9 0.0 copy-start.4
  5.9 0.7 %copy-done.4 = f32[4]{0:T(128)S(1)} copy-done((f32[4]{0:T(128)S(1)}, f32[4]{0:T(128)}, u32[]{:S(2)}) %copy-start.4) | copy-done | bytes 40
  6.6 19.9 %transform.1 = (f32[30,64,64]{2,1,0:T(8,128)S(1)}, f32[128,2048]{1,0:T(8,128)S(1)}, bf16[128,1552]{1,0:T(8,128)(2,1)S(1)}, bf16[128,128]{1,0:T(8,128)(2,1)S(1)}, bf16[128,128]{1,0:T(8,128)(2,1)S(1)}) custom-call(s32[2,2,8]{2,1,0:T(2,128)S(1)} %bitcast.16, s32[8,2,2,8]{3,2,1,0:T(2,128)S(1)} %bitcast.15, f32[4]{0:T(128)S(1)} %copy-done.4, ...), custom_call_target="tpu_custom_call" | custom-call | tf_op jit(solution)/shard_map/transform/pallas_call | solution.py:376
  26.5 1.6 %write_out.1 = (f32[30,64,64]{2,1,0:T(8,128)}, f32[128,3600]{1,0:T(8,128)}) custom-call(f32[30,64,64]{2,1,0:T(8,128)S(1)} %get-tuple-element.9.spectrum_in, f32[128,2048]{1,0:T(8,128)S(1)} %get-tuple-element.10.grid_in, bf16[128,1552]{1,0:T(8,128)(2,1)S(1)} %get-tuple-element.11.rest_ref, bf16[128,128]{1,0:T(8,128)(2,1)S(1)} %get-tuple-element.12.high_ref, ...), custom_call_target="tpu_custom_call" | custom-call | tf_op jit(solution)/shard_map/write_out/pallas_call | solution.py:422
  (1 shorter events, 0.0 us)
Async XLA Ops:
  2.0 1.5 %copy-start = (f32[2,4,16,3600]{3,2,1,0:T(8,128)S(1)}, f32[2,4,16,3600]{3,2,1,0:T(8,128)}, u32[]{:S(2)}) copy-start(f32[2,4,16,3600]{3,2,1,0:T(8,128)} %param.6) | copy-start | bytes 5529604
  3.5 1.0 %copy-start.1 = (bf16[1,1,30,2,32,64]{5,4,3,2,1,0:T(8,128)(2,1)S(1)}, bf16[1,1,30,2,32,64]{5,4,3,2,1,0:T(8,128)(2,1)}, u32[]{:S(2)}) copy-start(bf16[1,1,30,2,32,64]{5,4,3,2,1,0:T(8,128)(2,1)} %param.11) | copy-start | bytes 737284
  4.5 0.7 %copy-start.2 = (s32[8,2,8,2]{2,3,1,0:T(2,128)S(1)}, s32[8,2,8,2]{2,3,1,0:T(2,128)}, u32[]{:S(2)}) copy-start(s32[8,2,8,2]{2,3,1,0:T(2,128)} %param.9) | copy-start | bytes 3076
  5.2 0.7 %copy-start.3 = (s32[2,8,2]{1,2,0:T(2,128)S(1)}, s32[2,8,2]{1,2,0:T(2,128)}, u32[]{:S(2)}) copy-start(s32[2,8,2]{1,2,0:T(2,128)} %param.8) | copy-start | bytes 388
  5.9 0.7 %copy-start.4 = (f32[4]{0:T(128)S(1)}, f32[4]{0:T(128)}, u32[]{:S(2)}) copy-start(f32[4]{0:T(128)} %weight_hbm.1) | copy-start | bytes 52

commit v4 on v3

--- a/solution.py
+++ b/solution.py
@@ -318,6 +318,10 @@
         d = place(t, dest_count, me)
         fold_copy(d, spec, lat).wait_send()
         syn_copy(d, me).wait_send()
+
+
+def stay(array):
+    return pltpu.with_memory_space_constraint(array, pltpu.HBM)
 
 
 def write_kernel(spectrum_in, grid_in, rest_ref, high_ref, low_ref, spectrum_ref, grid_ref, buf, sem):
@@ -412,12 +416,12 @@
         ),
         name="transform",
     )(
-        jnp.transpose(owner_waves, (0, 2, 1)),
-        jnp.transpose(skip_blocks, (0, 1, 3, 2)),
-        quad_weight,
-        field_grid.reshape(LANES, length),
+        stay(jnp.transpose(owner_waves, (0, 2, 1))),
+        stay(jnp.transpose(skip_blocks, (0, 1, 3, 2))),
+        stay(quad_weight),
+        stay(field_grid.reshape(LANES, length)),
         table,
-        given_spectrum.reshape(slots, columns, KB),
+        stay(given_spectrum.reshape(slots, columns, KB)),
     )
     spectrum, back_grid = pl.pallas_call(
         write_kernel,

time: 28.4 us -> 23.2 us (0.82)
  local copies, waits for them, and re-layouts: 5.93 us -> 1.33 us
  Pallas kernels: 21.5 us -> 21 us
    unnamed x10 -> x0, local copies, waits for them, and re-layouts: 4.6 us -> none
    pallas_call x1, Pallas kernels: 19.9 us -> 19.4 us  [on_device(): pl.pallas_call(functools.partial(kernel, lat_count, spec_count), out_shap...]
where the time goes in v4:
time: 23.2 us; the launch traced here: 23 us
  Pallas kernels  21 us (91%)
  local copies, waits for them, and re-layouts  1.33 us (6%)
  between operations  0.65 us (3%)
    pallas_call x1, Pallas kernels, on_device(): pl.pallas_call(functools.partial(kernel, lat_count, spec_count), out_shap...  19.4 us
    pallas_call x1, Pallas kernels, on_device(): pl.pallas_call(write_kernel, out_shape=(jax.ShapeDtypeStruct((slots, colu...  1.62 us
    pad x1, local copies, waits for them, and re-layouts, on_device(): jnp.pad(table, ((0, 0), (0, quarters * per_wide - slots), (0, 0), (0, 0)))  1.08 us

profile of v4, /device:TPU:0, one launch (start us, length us, event | category | flops | bytes accessed | tf_op | source)
XLA Modules:
  0.0 23.0 jit_solution(12012662672286395014)
XLA Ops:
  0.6 1.1 %pad.4 = bf16[8,32,4,64]{3,2,1,0:T(4,128)(2,1)S(1)} pad(bf16[8,30,4,64]{3,2,1,0:T(4,128)(2,1)} %bitcast.17, bf16[]{:T(256)} %constant.2.clone.1), padding=0_0x0_2x0_0x0_0 | pad | bytes 253954 | tf_op jit(solution)/shard_map/jit(_pad)/pad | solution.py:367
  1.8 0.2 reshape.24.table_ref
  2.0 19.4 %transform.1 = (f32[30,64,64]{2,1,0:T(8,128)S(1)}, f32[128,2048]{1,0:T(8,128)S(1)}, bf16[128,1552]{1,0:T(8,128)(2,1)S(1)}, bf16[128,128]{1,0:T(8,128)(2,1)S(1)}, bf16[128,128]{1,0:T(8,128)(2,1)S(1)}) custom-call(s32[2,2,8]{2,1,0:T(2,128)} %bitcast.19, s32[8,2,2,8]{3,2,1,0:T(2,128)} %bitcast.18, f32[4]{0:T(128)} %weight_hbm.1, f32[128,3600]{1,0:T(8,128)} %bitcast.13, ...), custom_call_target="tpu_custom_call" | custom-call | tf_op jit(solution)/shard_map/transform/pallas_call | solution.py:380
  21.4 1.6 %write_out.1 = (f32[30,64,64]{2,1,0:T(8,128)}, f32[128,3600]{1,0:T(8,128)}) custom-call(f32[30,64,64]{2,1,0:T(8,128)S(1)} %get-tuple-element.9.spectrum_in, f32[128,2048]{1,0:T(8,128)S(1)} %get-tuple-element.10.grid_in, bf16[128,1552]{1,0:T(8,128)(2,1)S(1)} %get-tuple-element.11.rest_ref, bf16[128,128]{1,0:T(8,128)(2,1)S(1)} %get-tuple-element.12.high_ref, ...), custom_call_target="tpu_custom_call" | custom-call | tf_op jit(solution)/shard_map/write_out/pallas_call | solution.py:426
  (1 shorter events, 0.0 us)

commit v5 on v4

--- a/solution.py
+++ b/solution.py
@@ -45,7 +45,7 @@
     skip_hbm,
     weight_hbm,
     field_ref,
-    table_ref,
+    table_hbm,
     given_hbm,
     spectrum_ref,
     grid_ref,
@@ -56,6 +56,9 @@
     skip_ref,
     weight_ref,
     given_ref,
+    table_raw,
+    table_stage,
+    table_ref,
     field_buf,
     table_recv,
     stage,
@@ -87,67 +90,59 @@
     spec = lax.axis_index("spec")
     me = spec * lat_count + lat
 
-    def place(t, n, mine):
-        return lax.rem(mine + t, n)
-
-    def device(d):
-        return {"spec": d // lat_count, "lat": lax.rem(d, lat_count)}
+    lats = [lat] + [lax.rem(lat + t, lat_count) for t in range(1, lat_count)]
+    specs = [spec] + [lax.rem(spec + t, spec_count) for t in range(1, spec_count)]
+    others = [(q, b) for b in lats for q in specs][1:]
+
+    def finish(buf, blocks, sem):
+        part = buf.at[pl.ds(0, blocks * 16)]
+        pltpu.make_async_copy(part, part, sem).wait()
 
     waves_copy = pltpu.make_async_copy(waves_hbm, waves_ref, local_sem.at[0])
     skip_copy = pltpu.make_async_copy(skip_hbm, skip_ref, local_sem.at[1])
     weight_copy = pltpu.make_async_copy(weight_hbm, weight_ref, local_sem.at[2])
     given_copy = pltpu.make_async_copy(given_hbm, given_ref, local_sem.at[3])
     field_copy = pltpu.make_async_copy(field_ref, field_buf, local_sem.at[4])
+    table_move = pltpu.make_async_copy(table_hbm, table_raw, local_sem.at[5])
+    table_move.start()
+    barrier = pltpu.get_barrier_semaphore()
+    for q, b in others:
+        pl.semaphore_signal(
+            barrier, inc=1, device_id={"spec": q, "lat": b}, device_id_type=MESH
+        )
     for copy in (waves_copy, skip_copy, weight_copy, given_copy, field_copy):
         copy.start()
-    barrier = pltpu.get_barrier_semaphore()
-
-    @pl.loop(1, dest_count)
-    def _(t):
-        pl.semaphore_signal(
-            barrier, inc=1, device_id=device(place(t, dest_count, me)), device_id_type=MESH
-        )
-
+
+    table_move.wait()
+    per_row = WIDE // LANES
+
+    @pl.loop(0, lat_count)
+    def _(o):
+        for t in range(table_ref.shape[1] * 16 // (pair_dev * LANES)):
+            u, v = t // per_row, t % per_row
+            if 2 * t < slots:
+                both = jnp.concatenate(
+                    [table_raw[o, 2 * t].astype(f32), table_raw[o, 2 * t + 1].astype(f32)], axis=1
+                )
+            else:
+                both = jnp.zeros((pair_dev, LANES), f32)
+            table_stage[o, u * pair_dev : (u + 1) * pair_dev, v * LANES : (v + 1) * LANES] = both
+
+    table_ref[...] = table_stage[...].reshape(table_ref.shape).astype(bf16)
     pl.semaphore_wait(barrier, dest_count - 1)
-
-    def table_copy(to, slot):
-        return pltpu.make_async_remote_copy(
-            src_ref=table_ref.at[pl.ds(to * 16, 16)],
-            dst_ref=table_recv.at[pl.ds(slot * 16, 16)],
-            send_sem=table_send_sem.at[to],
-            recv_sem=table_recv_sem.at[slot],
-            device_id={"lat": to},
+    for b in lats[1:]:
+        pltpu.make_async_remote_copy(
+            src_ref=table_ref.at[pl.ds(b * 16, 16)],
+            dst_ref=table_recv.at[pl.ds(lat * 16, 16)],
+            send_sem=table_send_sem,
+            recv_sem=table_recv_sem,
+            device_id={"lat": b},
             device_id_type=MESH,
-        )
-
-    def fold_copy(to, from_spec, from_lat):
-        return pltpu.make_async_remote_copy(
-            src_ref=fold_send.at[pl.ds(to * 16, 16)],
-            dst_ref=fold_recv.at[from_spec, pl.ds(from_lat * 16, 16)],
-            send_sem=fold_send_sem.at[to],
-            recv_sem=fold_recv_sem.at[from_spec * lat_count + from_lat],
-            device_id=device(to),
-            device_id_type=MESH,
-        )
-
-    def syn_copy(to, slot):
-        return pltpu.make_async_remote_copy(
-            src_ref=syn_send.at[pl.ds(lax.rem(to, lat_count) * 16, 16)],
-            dst_ref=syn_recv.at[pl.ds(slot * 16, 16)],
-            send_sem=syn_send_sem.at[to],
-            recv_sem=syn_recv_sem.at[slot],
-            device_id=device(to),
-            device_id_type=MESH,
-        )
-
-    @pl.loop(1, lat_count)
-    def _(t):
-        table_copy(place(t, lat_count, lat), lat).start()
+        ).start()
 
     own = pl.ds(pl.multiple_of(lat * 16, 16), 16)
     mine = pl.ds(pl.multiple_of(me * 16, 16), 16)
     table_recv[own, :] = table_ref[own, :]
-
     for copy in (waves_copy, skip_copy, weight_copy):
         copy.wait()
 
@@ -186,6 +181,54 @@
     rest = coeffs.shape[1] - slots * KB
     coeffs[:, slots * KB :] = jnp.zeros((2 * columns, rest), bf16)
 
+    field_copy.wait()
+    cuts = list(range(0, full * LANES, WIDE)) + [full * LANES]
+    cuts = [(b, min(b + WIDE, full * LANES)) for b in cuts[:-1]] + (
+        [(full * LANES, length)] if full * LANES < length else []
+    )
+    total = jnp.zeros((4 * half, LANES), f32)
+    for begin, end in cuts:
+        high, low = split(field_buf[:, begin:end])
+        part = waves8[:, begin:end]
+        total = total + dot(part, high, ACROSS) + dot(part, low, ACROSS)
+    fourier = total[: 2 * half] + total[2 * half :]
+
+    lane = lax.broadcasted_iota(jnp.int32, (half, LANES), 1)
+    pair_of = (lane // channels) % pair_dev
+    weight = jnp.zeros((half, LANES), f32)
+    for j in range(pair_dev):
+        weight = jnp.where(pair_of == j, weight_ref[j], weight)
+    weight = weight * (1.0 / length)
+
+    def butterfly(value):
+        turned = pltpu.roll(value, LANES // 2, 1)
+        return (turned + jnp.where(lane < LANES // 2, value, -value)) * weight
+
+    folded = [butterfly(fourier[:half]), butterfly(fourier[half:])]
+    offsets = [r * spec_count * channels + spec * channels for r in range(2)]
+    for pj in range(2 * pair_dev):
+        placed = jnp.zeros((half, LANES), f32)
+        for r in range(2):
+            turned = pltpu.roll(
+                folded[r], lax.rem(offsets[r] + (LANES - pj * channels), LANES), 1
+            )
+            here = (lane >= offsets[r]) & (lane < offsets[r] + channels)
+            placed = jnp.where(here, turned, placed)
+        stage[pl.ds(pj, half, stride=2 * pair_dev), :] = placed
+    fold_send[...] = stage[...].astype(bf16)
+
+    for q, b in others:
+        pltpu.make_async_remote_copy(
+            src_ref=fold_send.at[pl.ds((q * lat_count + b) * 16, 16)],
+            dst_ref=fold_recv.at[pl.ds(me * 16, 16)],
+            send_sem=fold_send_sem,
+            recv_sem=fold_recv_sem,
+            device_id={"spec": q, "lat": b},
+            device_id_type=MESH,
+        ).start()
+
+    fold_recv[mine, :] = fold_send[mine, :]
+
     m0, m1 = waves_ref[spec, 0, lat], waves_ref[spec, 1, lat]
     start1 = KB * ((L + KB - m0) >> SHIFT)
     lows, highs = [], []
@@ -203,9 +246,7 @@
     pick_col = lax.broadcasted_iota(jnp.int32, (rows, lat_count * 16), 1)
     same_band = (pick_row // group) == (pick_col // 16)
 
-    @pl.loop(1, lat_count)
-    def _(t):
-        table_copy(lat, place(t, lat_count, lat)).wait_recv()
+    finish(table_recv, lat_count - 1, table_recv_sem)
 
     blocks = table_recv[...]
     for u in range(masked.shape[1] // WIDE):
@@ -223,57 +264,30 @@
     rounded = synthesis.astype(bf16).astype(f32)
     syn_send[...] = jnp.where(lane_q < columns, rounded, synthesis - rounded).astype(bf16)
 
-    @pl.loop(1, dest_count)
-    def _(t):
-        syn_copy(place(t, dest_count, me), me).start()
+    for q, b in others:
+        pltpu.make_async_remote_copy(
+            src_ref=syn_send.at[pl.ds(b * 16, 16)],
+            dst_ref=syn_recv.at[pl.ds(me * 16, 16)],
+            send_sem=syn_send_sem,
+            recv_sem=syn_recv_sem,
+            device_id={"spec": q, "lat": b},
+            device_id_type=MESH,
+        ).start()
 
     syn_recv[mine, :] = syn_send[own, :]
 
-    field_copy.wait()
-    cuts = list(range(0, full * LANES, WIDE)) + [full * LANES]
-    cuts = [(b, min(b + WIDE, full * LANES)) for b in cuts[:-1]] + (
-        [(full * LANES, length)] if full * LANES < length else []
-    )
-    total = jnp.zeros((4 * half, LANES), f32)
-    for begin, end in cuts:
-        high, low = split(field_buf[:, begin:end])
-        part = waves8[:, begin:end]
-        total = total + dot(part, high, ACROSS) + dot(part, low, ACROSS)
-    fourier = total[: 2 * half] + total[2 * half :]
-
-    lane = lax.broadcasted_iota(jnp.int32, (half, LANES), 1)
-    pair_of = (lane // channels) % pair_dev
-    weight = jnp.zeros((half, LANES), f32)
-    for j in range(pair_dev):
-        weight = jnp.where(pair_of == j, weight_ref[j], weight)
-    weight = weight * (1.0 / length)
-
-    def butterfly(value):
-        turned = pltpu.roll(value, LANES // 2, 1)
-        return (turned + jnp.where(lane < LANES // 2, value, -value)) * weight
-
-    folded = [butterfly(fourier[:half]), butterfly(fourier[half:])]
-    offsets = [r * spec_count * channels + spec * channels for r in range(2)]
-    for pj in range(2 * pair_dev):
-        placed = jnp.zeros((half, LANES), f32)
-        for r in range(2):
-            turned = pltpu.roll(
-                folded[r], lax.rem(offsets[r] + (LANES - pj * channels), LANES), 1
-            )
-            here = (lane >= offsets[r]) & (lane < offsets[r] + channels)
-            placed = jnp.where(here, turned, placed)
-        stage[pl.ds(pj, half, stride=2 * pair_dev), :] = placed
-    fold_send[...] = stage[...].astype(bf16)
-
-    @pl.loop(1, dest_count)
-    def _(t):
-        fold_copy(place(t, dest_count, me), spec, lat).start()
-
-    fold_recv[spec, own, :] = fold_send[mine, :]
-
-    @pl.loop(1, dest_count)
-    def _(t):
-        syn_copy(me, place(t, dest_count, me)).wait_recv()
+    finish(fold_recv, dest_count - 1, fold_recv_sem)
+    gathered = fold_recv[0:rows, :].astype(f32)
+    for q in range(1, spec_count):
+        gathered = gathered + fold_recv[q * rows : (q + 1) * rows, :].astype(f32)
+    folded_own = gathered.T[:columns].astype(bf16)
+    for u in range(masked.shape[1] // WIDE):
+        part = dot(folded_own, masked[:, u * WIDE : (u + 1) * WIDE])
+        for k in range(u * WIDE // KB, min((u + 1) * WIDE // KB, slots)):
+            at = k * KB - u * WIDE
+            spectrum_ref[k] = part[:, at : at + KB]
+
+    finish(syn_recv, dest_count - 1, syn_recv_sem)
 
     received = syn_recv[...].astype(f32)
     stage[...] = received + pltpu.roll(received, LANES // 2, 1)
@@ -294,30 +308,9 @@
             grid_ref[:, begin:end] = dot(high, part) + dot(low, part)
     rest_ref[...] = waves8[:, done:]
 
-    @pl.loop(1, dest_count)
-    def _(t):
-        d = place(t, dest_count, me)
-        fold_copy(me, d // lat_count, lax.rem(d, lat_count)).wait_recv()
-
-    gathered = fold_recv[0].astype(f32)
-    for q in range(1, spec_count):
-        gathered = gathered + fold_recv[q].astype(f32)
-    folded_own = gathered.T[:columns].astype(bf16)
-    for u in range(masked.shape[1] // WIDE):
-        part = dot(folded_own, masked[:, u * WIDE : (u + 1) * WIDE])
-        for k in range(u * WIDE // KB, min((u + 1) * WIDE // KB, slots)):
-            at = k * KB - u * WIDE
-            spectrum_ref[k] = part[:, at : at + KB]
-
-    @pl.loop(1, lat_count)
-    def _(t):
-        table_copy(place(t, lat_count, lat), lat).wait_send()
-
-    @pl.loop(1, dest_count)
-    def _(t):
-        d = place(t, dest_count, me)
-        fold_copy(d, spec, lat).wait_send()
-        syn_copy(d, me).wait_send()
+    finish(table_recv, lat_count - 1, table_send_sem)
+    finish(fold_recv, dest_count - 1, fold_send_sem)
+    finish(syn_recv, dest_count - 1, syn_send_sem)
 
 
 def stay(array):
@@ -361,16 +354,10 @@
     columns = 2 * given_spectrum.shape[4]
     dest_count = lat_count * spec_count
     rows = lat_count * 4 * pair_dev
-    per_wide = WIDE // KB
     quarters = 16 // pair_dev
-    table = legendre_table[0]
-    table = jnp.pad(table, ((0, 0), (0, quarters * per_wide - slots), (0, 0), (0, 0)))
-    table = table.reshape(lat_count, quarters, per_wide, pair_dev, KB)
-    table = jnp.transpose(table, (0, 1, 3, 2, 4)).reshape(lat_count * 16, WIDE)
     half = 2 * dest_count
     f32, bf16 = jnp.float32, jnp.bfloat16
     vmem = pl.BlockSpec(memory_space=pltpu.VMEM)
-    smem = pl.BlockSpec(memory_space=pltpu.SMEM)
     dma = pltpu.SemaphoreType.DMA
     hbm = pl.BlockSpec(memory_space=pltpu.HBM)
     done = (length // 2) // WIDE * WIDE + WIDE
@@ -386,30 +373,33 @@
             stack,
             stack,
         ),
-        in_specs=[hbm, hbm, hbm, hbm, vmem, hbm],
+        in_specs=[hbm] * 6,
         out_specs=(vmem,) * 5,
         scratch_shapes=[
             pltpu.SMEM((spec_count, 2, lat_count), jnp.int32),
             pltpu.SMEM((lat_count, spec_count, 2, lat_count), jnp.int32),
             pltpu.SMEM((pair_dev,), f32),
             pltpu.VMEM((slots, columns, KB), bf16),
+            pltpu.VMEM((lat_count, slots, pair_dev, KB), bf16),
+            pltpu.VMEM((lat_count, 16, WIDE), f32),
+            pltpu.VMEM((lat_count * 16, WIDE), bf16),
             pltpu.VMEM((LANES, length), f32),
             pltpu.VMEM((lat_count * 16, WIDE), bf16),
             pltpu.VMEM((dest_count * 16, LANES), f32),
             pltpu.VMEM((dest_count * 16, LANES), bf16),
-            pltpu.VMEM((spec_count, rows, LANES), bf16),
+            pltpu.VMEM((spec_count * rows, LANES), bf16),
             pltpu.VMEM((rows, LANES), bf16),
             pltpu.VMEM((dest_count * 16, LANES), bf16),
             pltpu.VMEM((4 * half, length), bf16),
             pltpu.VMEM((rows, quarters * WIDE), bf16),
             pltpu.VMEM((2 * columns, quarters * WIDE), bf16),
-            dma((5,)),
-            dma((lat_count,)),
-            dma((lat_count,)),
-            dma((dest_count,)),
-            dma((dest_count,)),
-            dma((dest_count,)),
-            dma((dest_count,)),
+            dma((6,)),
+            dma,
+            dma,
+            dma,
+            dma,
+            dma,
+            dma,
         ],
         compiler_params=pltpu.CompilerParams(
             collective_id=0, has_side_effects=True, vmem_limit_bytes=32 * 2**20
@@ -420,7 +410,7 @@
         stay(jnp.transpose(skip_blocks, (0, 1, 3, 2))),
         stay(quad_weight),
         stay(field_grid.reshape(LANES, length)),
-        table,
+        stay(legendre_table[0]),
         stay(given_spectrum.reshape(slots, columns, KB)),
     )
     spectrum, back_grid = pl.pallas_call(

time: 23.2 us -> 19.6 us (0.84)
  Pallas kernels: 21 us -> 18.9 us
  local copies, waits for them, and re-layouts: 1.33 us -> 0 us
    pallas_call x1, Pallas kernels: 19.4 us -> 17.2 us  [on_device(): pl.pallas_call(functools.partial(kernel, lat_count, spec_count), out_shap...]
    pad x1 -> x0, local copies, waits for them, and re-layouts: 1.08 us -> none  [on_device(): jnp.pad(table, ((0, 0), (0, quarters * per_wide - slots), (0, 0), (0, 0)))]
    reshape x2 -> x0, local copies, waits for them, and re-layouts: 0.25 us -> none  [the longest x1 0.21 us: on_device(): table = jnp.transpose(table, (0, 1, 3, 2, 4)).reshape(lat_count * 16, WIDE)]
where the time goes in v5:
time: 19.6 us; the launch traced here: 19.5 us
  Pallas kernels  18.9 us (96%)
  between operations  0.64 us (3%)
    pallas_call x1, Pallas kernels, on_device(): pl.pallas_call(functools.partial(kernel, lat_count, spec_count), out_shap...  17.2 us
    pallas_call x1, Pallas kernels, on_device(): pl.pallas_call(write_kernel, out_shape=(jax.ShapeDtypeStruct((slots, colu...  1.62 us

profile of v5, /device:TPU:0, one launch (start us, length us, event | category | flops | bytes accessed | tf_op | source)
XLA Modules:
  0.0 19.5 jit_solution(3893631231050201770)
XLA Ops:
  0.6 17.2 %transform.1 = (f32[30,64,64]{2,1,0:T(8,128)S(1)}, f32[128,2048]{1,0:T(8,128)S(1)}, bf16[128,1552]{1,0:T(8,128)(2,1)S(1)}, bf16[128,128]{1,0:T(8,128)(2,1)S(1)}, bf16[128,128]{1,0:T(8,128)(2,1)S(1)}) custom-call(s32[2,2,8]{2,1,0:T(2,128)} %bitcast.11, s32[8,2,2,8]{3,2,1,0:T(2,128)} %bitcast.10, f32[4]{0:T(128)} %weight_hbm.1, f32[128,3600]{1,0:T(8,128)} %bitcast.7, ...), custom_call_target="tpu_custom_call" | custom-call | tf_op jit(solution)/shard_map/transform/pallas_call | solution.py:367
  17.9 1.6 %write_out.1 = (f32[30,64,64]{2,1,0:T(8,128)}, f32[128,3600]{1,0:T(8,128)}) custom-call(f32[30,64,64]{2,1,0:T(8,128)S(1)} %get-tuple-element.9.spectrum_in, f32[128,2048]{1,0:T(8,128)S(1)} %get-tuple-element.10.grid_in, bf16[128,1552]{1,0:T(8,128)(2,1)S(1)} %get-tuple-element.11.rest_ref, bf16[128,128]{1,0:T(8,128)(2,1)S(1)} %get-tuple-element.12.high_ref, ...), custom_call_target="tpu_custom_call" | custom-call | tf_op jit(solution)/shard_map/write_out/pallas_call | solution.py:416

commit v6 on v5

--- a/solution.py
+++ b/solution.py
@@ -48,10 +48,8 @@
     table_hbm,
     given_hbm,
     spectrum_ref,
-    grid_ref,
-    rest_ref,
-    high_ref,
-    low_ref,
+    waves8,
+    back_ref,
     waves_ref,
     skip_ref,
     weight_ref,
@@ -66,7 +64,6 @@
     fold_recv,
     syn_send,
     syn_recv,
-    waves8,
     masked,
     coeffs,
     local_sem,
@@ -170,8 +167,8 @@
         width = min(LANES, length - a * LANES)
         part = turn_c[:, a : a + 1] * base_c - turn_s[:, a : a + 1] * base_s
         high, low = split(part)
-        waves8[0 : 2 * half, a * LANES : a * LANES + width] = high[:, :width]
-        waves8[2 * half : 4 * half, a * LANES : a * LANES + width] = low[:, :width]
+        for n, piece in enumerate((high, low, high, low)):
+            waves8[2 * half * n : 2 * half * (n + 1), a * LANES : a * LANES + width] = piece[:, :width]
 
     given_copy.wait()
     for pair in range(slots // 2):
@@ -189,7 +186,7 @@
     total = jnp.zeros((4 * half, LANES), f32)
     for begin, end in cuts:
         high, low = split(field_buf[:, begin:end])
-        part = waves8[:, begin:end]
+        part = waves8[0 : 4 * half, begin:end]
         total = total + dot(part, high, ACROSS) + dot(part, low, ACROSS)
     fourier = total[: 2 * half] + total[2 * half :]
 
@@ -299,14 +296,7 @@
             back[r] = jnp.where((lane // channels) == pj, turned, back[r])
     back = jnp.concatenate([butterfly(back[0]), butterfly(back[1])], axis=0)
     high, low = split(jnp.concatenate([back, back], axis=0).T)
-    high_ref[...] = high
-    low_ref[...] = low
-    done = grid_ref.shape[1]
-    for begin, end in cuts:
-        if end <= done:
-            part = waves8[:, begin:end]
-            grid_ref[:, begin:end] = dot(high, part) + dot(low, part)
-    rest_ref[...] = waves8[:, done:]
+    back_ref[...] = jnp.concatenate([high, low], axis=1)
 
     finish(table_recv, lat_count - 1, table_send_sem)
     finish(fold_recv, dest_count - 1, fold_send_sem)
@@ -317,28 +307,20 @@
     return pltpu.with_memory_space_constraint(array, pltpu.HBM)
 
 
-def write_kernel(spectrum_in, grid_in, rest_ref, high_ref, low_ref, spectrum_ref, grid_ref, buf, sem):
-    done = grid_in.shape[1]
+def write_kernel(spectrum_in, waves8, back_ref, spectrum_ref, grid_ref, buf, sem):
     length = grid_ref.shape[1]
-    copies = [
-        pltpu.make_async_copy(grid_in, grid_ref.at[:, pl.ds(0, done)], sem.at[0]),
-        pltpu.make_async_copy(spectrum_in, spectrum_ref, sem.at[1]),
-    ]
-    for copy in copies:
-        copy.start()
-    high, low = high_ref[...], low_ref[...]
-    for n, begin in enumerate(range(0, length - done, WIDE)):
-        end = min(begin + WIDE, length - done)
-        if length - done - end < LANES:
-            end = length - done
-        if begin >= end or n >= sem.shape[0] - 2:
-            break
-        part = rest_ref[:, begin:end]
-        buf[:, begin:end] = dot(high, part) + dot(low, part)
+    copies = [pltpu.make_async_copy(spectrum_in, spectrum_ref, sem.at[0])]
+    copies[0].start()
+    back = back_ref[...]
+    parts = sem.shape[0] - 1
+    for n in range(parts):
+        begin = n * WIDE
+        end = length if n == parts - 1 else begin + WIDE
+        buf[:, begin:end] = dot(back, waves8[:, begin:end])
         copy = pltpu.make_async_copy(
             buf.at[:, pl.ds(begin, end - begin)],
-            grid_ref.at[:, pl.ds(done + begin, end - begin)],
-            sem.at[2 + n],
+            grid_ref.at[:, pl.ds(begin, end - begin)],
+            sem.at[1 + n],
         )
         copy.start()
         copies.append(copy)
@@ -360,21 +342,15 @@
     vmem = pl.BlockSpec(memory_space=pltpu.VMEM)
     dma = pltpu.SemaphoreType.DMA
     hbm = pl.BlockSpec(memory_space=pltpu.HBM)
-    done = (length // 2) // WIDE * WIDE + WIDE
-    rest = length - done
-    parts = rest // WIDE + (1 if rest % WIDE >= LANES else 0)
-    stack = jax.ShapeDtypeStruct((LANES, 4 * half), bf16)
-    spectrum, first, waves_rest, high, low = pl.pallas_call(
+    spectrum, wave_table, back = pl.pallas_call(
         functools.partial(kernel, lat_count, spec_count),
         out_shape=(
             jax.ShapeDtypeStruct((slots, columns, KB), f32),
-            jax.ShapeDtypeStruct((LANES, done), f32),
-            jax.ShapeDtypeStruct((4 * half, rest), bf16),
-            stack,
-            stack,
+            jax.ShapeDtypeStruct((8 * half, length), bf16),
+            jax.ShapeDtypeStruct((LANES, 8 * half), bf16),
         ),
         in_specs=[hbm] * 6,
-        out_specs=(vmem,) * 5,
+        out_specs=(vmem,) * 3,
         scratch_shapes=[
             pltpu.SMEM((spec_count, 2, lat_count), jnp.int32),
             pltpu.SMEM((lat_count, spec_count, 2, lat_count), jnp.int32),
@@ -390,7 +366,6 @@
             pltpu.VMEM((spec_count * rows, LANES), bf16),
             pltpu.VMEM((rows, LANES), bf16),
             pltpu.VMEM((dest_count * 16, LANES), bf16),
-            pltpu.VMEM((4 * half, length), bf16),
             pltpu.VMEM((rows, quarters * WIDE), bf16),
             pltpu.VMEM((2 * columns, quarters * WIDE), bf16),
             dma((6,)),
@@ -419,12 +394,12 @@
             jax.ShapeDtypeStruct((slots, columns, KB), f32),
             jax.ShapeDtypeStruct((LANES, length), f32),
         ),
-        in_specs=[vmem] * 5,
+        in_specs=[vmem] * 3,
         out_specs=(hbm, hbm),
-        scratch_shapes=[pltpu.VMEM((LANES, rest), f32), dma((2 + parts,))],
+        scratch_shapes=[pltpu.VMEM((LANES, length), f32), dma((1 + length // WIDE,))],
         compiler_params=pltpu.CompilerParams(vmem_limit_bytes=16 * 2**20),
         name="write_out",
-    )(spectrum, first, waves_rest, high, low)
+    )(spectrum, wave_table, back)
     return (spectrum.reshape(given_spectrum.shape), back_grid.reshape(field_grid.shape))
 
 

time: 19.6 us -> 19.3 us (0.985)
  Pallas kernels: 18.9 us -> 18.5 us
    pallas_call x1, Pallas kernels: 17.2 us -> 16.8 us  [on_device(): pl.pallas_call(functools.partial(kernel, lat_count, spec_count), out_shap...]
where the time goes in v6:
time: 19.3 us; the launch traced here: 19.1 us
  Pallas kernels  18.5 us (96%)
  between operations  0.64 us (3%)
    pallas_call x1, Pallas kernels, on_device(): pl.pallas_call(functools.partial(kernel, lat_count, spec_count), out_shap...  16.8 us
    pallas_call x1, Pallas kernels, on_device(): pl.pallas_call(write_kernel, out_shape=(jax.ShapeDtypeStruct((slots, colu...  1.65 us

profile of v6, /device:TPU:0, one launch (start us, length us, event | category | flops | bytes accessed | tf_op | source)
XLA Modules:
  0.0 19.1 jit_solution(16778309538641182372)
XLA Ops:
  0.6 16.8 %transform.1 = (f32[30,64,64]{2,1,0:T(8,128)S(1)}, bf16[256,3600]{1,0:T(8,128)(2,1)S(1)}, bf16[128,256]{1,0:T(8,128)(2,1)S(1)}) custom-call(s32[2,2,8]{2,1,0:T(2,128)} %bitcast.11, s32[8,2,2,8]{3,2,1,0:T(2,128)} %bitcast.10, f32[4]{0:T(128)} %weight_hbm.1, f32[128,3600]{1,0:T(8,128)} %bitcast.7, bf16[8,30,4,64]{3,2,1,0:T(4,128)(2,1)} %bitcast.9, ...), custom_call_target="tpu_custom_call" | custom-call | tf_op jit(solution)/shard_map/transform/pallas_call | solution.py:345
  17.5 1.7 %write_out.1 = (f32[30,64,64]{2,1,0:T(8,128)}, f32[128,3600]{1,0:T(8,128)}) custom-call(f32[30,64,64]{2,1,0:T(8,128)S(1)} %get-tuple-element.7.spectrum_in, bf16[256,3600]{1,0:T(8,128)(2,1)S(1)} %get-tuple-element.8.waves8, bf16[128,256]{1,0:T(8,128)(2,1)S(1)} %get-tuple-element.9.back_ref), custom_call_target="tpu_custom_call" | custom-call | tf_op jit(solution)/shard_map/write_out/pallas_call | solution.py:391

commit v7 on v6

--- a/solution.py
+++ b/solution.py
@@ -190,42 +190,6 @@
         total = total + dot(part, high, ACROSS) + dot(part, low, ACROSS)
     fourier = total[: 2 * half] + total[2 * half :]
 
-    lane = lax.broadcasted_iota(jnp.int32, (half, LANES), 1)
-    pair_of = (lane // channels) % pair_dev
-    weight = jnp.zeros((half, LANES), f32)
-    for j in range(pair_dev):
-        weight = jnp.where(pair_of == j, weight_ref[j], weight)
-    weight = weight * (1.0 / length)
-
-    def butterfly(value):
-        turned = pltpu.roll(value, LANES // 2, 1)
-        return (turned + jnp.where(lane < LANES // 2, value, -value)) * weight
-
-    folded = [butterfly(fourier[:half]), butterfly(fourier[half:])]
-    offsets = [r * spec_count * channels + spec * channels for r in range(2)]
-    for pj in range(2 * pair_dev):
-        placed = jnp.zeros((half, LANES), f32)
-        for r in range(2):
-            turned = pltpu.roll(
-                folded[r], lax.rem(offsets[r] + (LANES - pj * channels), LANES), 1
-            )
-            here = (lane >= offsets[r]) & (lane < offsets[r] + channels)
-            placed = jnp.where(here, turned, placed)
-        stage[pl.ds(pj, half, stride=2 * pair_dev), :] = placed
-    fold_send[...] = stage[...].astype(bf16)
-
-    for q, b in others:
-        pltpu.make_async_remote_copy(
-            src_ref=fold_send.at[pl.ds((q * lat_count + b) * 16, 16)],
-            dst_ref=fold_recv.at[pl.ds(me * 16, 16)],
-            send_sem=fold_send_sem,
-            recv_sem=fold_recv_sem,
-            device_id={"spec": q, "lat": b},
-            device_id_type=MESH,
-        ).start()
-
-    fold_recv[mine, :] = fold_send[mine, :]
-
     m0, m1 = waves_ref[spec, 0, lat], waves_ref[spec, 1, lat]
     start1 = KB * ((L + KB - m0) >> SHIFT)
     lows, highs = [], []
@@ -273,16 +237,41 @@
 
     syn_recv[mine, :] = syn_send[own, :]
 
-    finish(fold_recv, dest_count - 1, fold_recv_sem)
-    gathered = fold_recv[0:rows, :].astype(f32)
-    for q in range(1, spec_count):
-        gathered = gathered + fold_recv[q * rows : (q + 1) * rows, :].astype(f32)
-    folded_own = gathered.T[:columns].astype(bf16)
-    for u in range(masked.shape[1] // WIDE):
-        part = dot(folded_own, masked[:, u * WIDE : (u + 1) * WIDE])
-        for k in range(u * WIDE // KB, min((u + 1) * WIDE // KB, slots)):
-            at = k * KB - u * WIDE
-            spectrum_ref[k] = part[:, at : at + KB]
+    lane = lax.broadcasted_iota(jnp.int32, (half, LANES), 1)
+    pair_of = (lane // channels) % pair_dev
+    weight = jnp.zeros((half, LANES), f32)
+    for j in range(pair_dev):
+        weight = jnp.where(pair_of == j, weight_ref[j], weight)
+    weight = weight * (1.0 / length)
+
+    def butterfly(value):
+        turned = pltpu.roll(value, LANES // 2, 1)
+        return (turned + jnp.where(lane < LANES // 2, value, -value)) * weight
+
+    folded = [butterfly(fourier[:half]), butterfly(fourier[half:])]
+    offsets = [r * spec_count * channels + spec * channels for r in range(2)]
+    for pj in range(2 * pair_dev):
+        placed = jnp.zeros((half, LANES), f32)
+        for r in range(2):
+            turned = pltpu.roll(
+                folded[r], lax.rem(offsets[r] + (LANES - pj * channels), LANES), 1
+            )
+            here = (lane >= offsets[r]) & (lane < offsets[r] + channels)
+            placed = jnp.where(here, turned, placed)
+        stage[pl.ds(pj, half, stride=2 * pair_dev), :] = placed
+    fold_send[...] = stage[...].astype(bf16)
+
+    for q, b in others:
+        pltpu.make_async_remote_copy(
+            src_ref=fold_send.at[pl.ds((q * lat_count + b) * 16, 16)],
+            dst_ref=fold_recv.at[pl.ds(me * 16, 16)],
+            send_sem=fold_send_sem,
+            recv_sem=fold_recv_sem,
+            device_id={"spec": q, "lat": b},
+            device_id_type=MESH,
+        ).start()
+
+    fold_recv[mine, :] = fold_send[mine, :]
 
     finish(syn_recv, dest_count - 1, syn_recv_sem)
 
@@ -297,6 +286,17 @@
     back = jnp.concatenate([butterfly(back[0]), butterfly(back[1])], axis=0)
     high, low = split(jnp.concatenate([back, back], axis=0).T)
     back_ref[...] = jnp.concatenate([high, low], axis=1)
+
+    finish(fold_recv, dest_count - 1, fold_recv_sem)
+    gathered = fold_recv[0:rows, :].astype(f32)
+    for q in range(1, spec_count):
+        gathered = gathered + fold_recv[q * rows : (q + 1) * rows, :].astype(f32)
+    folded_own = gathered.T[:columns].astype(bf16)
+    for u in range(masked.shape[1] // WIDE):
+        part = dot(folded_own, masked[:, u * WIDE : (u + 1) * WIDE])
+        for k in range(u * WIDE // KB, min((u + 1) * WIDE // KB, slots)):
+            at = k * KB - u * WIDE
+            spectrum_ref[k] = part[:, at : at + KB]
 
     finish(table_recv, lat_count - 1, table_send_sem)
     finish(fold_recv, dest_count - 1, fold_send_sem)

time: 19.3 us -> 19.6 us (1.016)
  Pallas kernels: 18.5 us -> 18.9 us
    pallas_call x1, Pallas kernels: 16.8 us -> 17.2 us  [on_device(): pl.pallas_call(functools.partial(kernel, lat_count, spec_count), out_shap...]
where the time goes in v7:
time: 19.6 us; the launch traced here: 19.5 us
  Pallas kernels  18.9 us (96%)
  between operations  0.64 us (3%)
    pallas_call x1, Pallas kernels, on_device(): pl.pallas_call(functools.partial(kernel, lat_count, spec_count), out_shap...  17.2 us
    pallas_call x1, Pallas kernels, on_device(): pl.pallas_call(write_kernel, out_shape=(jax.ShapeDtypeStruct((slots, colu...  1.65 us

profile of v7, /device:TPU:0, one launch (start us, length us, event | category | flops | bytes accessed | tf_op | source)
XLA Modules:
  0.0 19.5 jit_solution(5458731029057590062)
XLA Ops:
  0.6 17.2 %transform.1 = (f32[30,64,64]{2,1,0:T(8,128)S(1)}, bf16[256,3600]{1,0:T(8,128)(2,1)S(1)}, bf16[128,256]{1,0:T(8,128)(2,1)S(1)}) custom-call(s32[2,2,8]{2,1,0:T(2,128)} %bitcast.11, s32[8,2,2,8]{3,2,1,0:T(2,128)} %bitcast.10, f32[4]{0:T(128)} %weight_hbm.1, f32[128,3600]{1,0:T(8,128)} %bitcast.7, bf16[8,30,4,64]{3,2,1,0:T(4,128)(2,1)} %bitcast.9, ...), custom_call_target="tpu_custom_call" | custom-call | tf_op jit(solution)/shard_map/transform/pallas_call | solution.py:345
  17.8 1.7 %write_out.1 = (f32[30,64,64]{2,1,0:T(8,128)}, f32[128,3600]{1,0:T(8,128)}) custom-call(f32[30,64,64]{2,1,0:T(8,128)S(1)} %get-tuple-element.7.spectrum_in, bf16[256,3600]{1,0:T(8,128)(2,1)S(1)} %get-tuple-element.8.waves8, bf16[128,256]{1,0:T(8,128)(2,1)S(1)} %get-tuple-element.9.back_ref), custom_call_target="tpu_custom_call" | custom-call | tf_op jit(solution)/shard_map/write_out/pallas_call | solution.py:391
